TPU v7x, 256 devices: a whole 4x4x8 slice. The times are simulated.
256 devices in a mesh: dp: 128 (over z, x, y), mp: 2 (over core).
Axes of the slice: x: 4, y: 4, z: 8, core: 2. Of those that a mesh axis runs over, the one named last changes fastest.
Arguments:
- gradient: float32 [131072, 512], P('dp', 'mp'), may hold values from -12 to 12
- moment: float32 [131072, 512], P('dp', 'mp'), may hold values from 0.01 to 1
- left_stat: float32 [128, 1024, 1024], P('dp', 'mp'), may hold values from -1 to 3
- right_stat: float32 [128, 512, 512], P('dp', 'mp'), may hold values from -1 to 3
- left_root: bfloat16 [128, 1024, 1024], P('dp'), may hold values from -1 to 5
- right_root: bfloat16 [128, 512, 512], P('dp', None, 'mp'), may hold values from -1 to 5
- seg_block: int32 [131072], P('dp'), may hold values from 0 to 127, as said below
- seg_row: int32 [131072], P('dp'), may hold values from 0 to 1023, as said below
- owner_table: int32 [128], replicated, may hold values from 0 to 127, as said below
Outputs:
- update: bfloat16 [131072, 512], P('dp', 'mp')
- moment_new: float32 [131072, 512], P('dp', 'mp')
- left_new: float32 [128, 1024, 1024], P('dp', 'mp')
- right_new: float32 [128, 512, 512], P('dp', 'mp')
Inputs may be any that keep to these rules, and one draw needn't show every extreme that they name: `seg_block`: over all devices, every block's rows 0 to 1023 each appear exactly once. The rows of one device hold at most 12 rows of one block, and some device holds exactly 12 rows of some block in every draw. Every row of one device belongs to a block whose owner differs from the device by the same amount for as many rows on every device; each owner receives 1024 rows. `seg_row`: together with seg_block, names each block row exactly once. `owner_table`: each device owns exactly one block.
All inputs are finite; a program needn't handle non-finite values.
Results may differ from a plain program's by a relative error of at most 0.0058.
Values may be sent and summed in bfloat16 or wider, within the bound.
No kernel may reach another device: no remote copies, remote signals or barrier semaphores. Data moves between devices by JAX's collectives and lax.ppermute only.
A program may use at most 64 MiB of HBM per device.

v0:
```python
import jax
import jax.numpy as jnp
from jax import lax
from jax.sharding import PartitionSpec as P

GRAM_DECAY = 0.95
MOMENT_DECAY = 0.99
ADAM_EPS = 1e-08
GRAFT_EPS = 1e-06


def body(
    gradient, moment, left_stat, right_stat, left_root, right_root, seg_block, seg_row, owner_table
):
    owners_count = lax.axis_size("dp")
    block_rows = gradient.shape[0]
    capacity = 3 * block_rows // (2 * owners_count)
    own_index = lax.axis_index("dp")
    core_index = lax.axis_index("mp")
    moment_new = MOMENT_DECAY * moment + (1.0 - MOMENT_DECAY) * gradient * gradient
    adam_step = gradient / (jnp.sqrt(moment_new) + ADAM_EPS)
    seg_sq = jnp.sum(adam_step * adam_step, axis=1)
    block_ids = jnp.arange(owner_table.shape[0], dtype=jnp.int32)
    matches = seg_block[:, None] == block_ids[None, :]
    target = jnp.sum(jnp.where(matches, owner_table[None, :], 0), axis=1)
    owner_ids = jnp.arange(owners_count, dtype=jnp.int32)
    onehot = (target[:, None] == owner_ids[None, :]).astype(jnp.int32)
    slot_index = jnp.sum((jnp.cumsum(onehot, axis=0) - onehot) * onehot, axis=1)
    sending = lax.all_gather(gradient, "mp", axis=1, tiled=True)
    row_width = sending.shape[1]
    send_rows = (
        jnp.zeros((owners_count, capacity, row_width), jnp.float32)
        .at[target, slot_index]
        .set(sending)
    )
    send_pos = (
        jnp.full((owners_count, capacity), block_rows, jnp.int32)
        .at[target, slot_index]
        .set(seg_row)
    )
    partial_sums = jnp.sum(jnp.where(matches, seg_sq[:, None], 0.0), axis=0)
    got_rows, got_pos = (
        lax.all_to_all(send_rows, "dp", split_axis=0, concat_axis=0, tiled=True),
        lax.all_to_all(send_pos, "dp", split_axis=0, concat_axis=0, tiled=True),
    )
    totals = lax.psum(partial_sums, ("dp", "mp"))
    adam_total = jnp.sum(jnp.where(owner_table == own_index, totals, 0.0))
    flat_pos = got_pos.reshape(-1)
    gathered = (
        jnp.zeros((block_rows, row_width), jnp.float32)
        .at[flat_pos]
        .set(got_rows.reshape(-1, row_width), mode="drop")
    )
    half_rows = left_stat.shape[1]
    half_cols = right_stat.shape[1]
    own_rows = lax.dynamic_slice_in_dim(gathered, core_index * half_rows, half_rows, 0)
    own_cols = lax.dynamic_slice_in_dim(gathered, core_index * half_cols, half_cols, 1)
    left_gram = lax.dot_general(
        own_rows,
        gathered,
        (((1,), (1,)), ((), ())),
        precision=lax.Precision.HIGHEST,
        preferred_element_type=jnp.float32,
    )
    right_gram = lax.dot_general(
        own_cols,
        gathered,
        (((0,), (0,)), ((), ())),
        precision=lax.Precision.HIGHEST,
        preferred_element_type=jnp.float32,
    )
    left_new = GRAM_DECAY * left_stat[0] + left_gram
    right_new = GRAM_DECAY * right_stat[0] + right_gram
    coarse = gathered.astype(jnp.bfloat16)
    mixed = jnp.dot(coarse, right_root[0], preferred_element_type=jnp.float32).astype(jnp.bfloat16)
    precond = jnp.dot(left_root[0], mixed, preferred_element_type=jnp.float32)
    precond_part = jnp.sum(precond * precond)
    precond_total = lax.psum(precond_part, "mp")
    graft_scale = jnp.sqrt(adam_total) / (jnp.sqrt(precond_total) + GRAFT_EPS)
    grafted = (precond * graft_scale).astype(jnp.bfloat16)
    returning = jnp.take(grafted, got_pos, axis=0, mode="fill", fill_value=0)
    returned = lax.all_to_all(returning, "dp", split_axis=0, concat_axis=0, tiled=True)
    update = returned[target, slot_index]
    return (update, moment_new, left_new[None], right_new[None])


def solution(mesh):
    in_specs = (
        P("dp", "mp"),
        P("dp", "mp"),
        P("dp", "mp", None),
        P("dp", "mp", None),
        P("dp", None, None),
        P("dp", None, "mp"),
        P("dp"),
        P("dp"),
        P(),
    )
    out_specs = (P("dp", "mp"), P("dp", "mp"), P("dp", "mp", None), P("dp", "mp", None))
    return jax.shard_map(body, mesh=mesh, in_specs=in_specs, out_specs=out_specs, check_vma=False)
```

profile of v0, /device:TPU:2, one launch (start us, length us, event | category | flops | bytes accessed | tf_op | source)
XLA Modules:
  0.0 288.1 jit_solution(15315267188024985165)
XLA Ops:
  7.9 1.1 select_reduce_fusion.1
  10.1 4.5 %scatter_custom_fusion.1 = s32[1536]{0:T(1024)S(1)} fusion(s32[1024]{0:T(1024)S(1)} %broadcast_select_fusion.1, s32[1024]{0:T(1024)} %param.16, s32[]{:T(128)} %constant.16.clone.1), kind=kCustom, calls=%fused_computation.52 | custom fusion | bytes 6656
  15.3 15.4 %all-to-all-start = ((s32[128,1,12]{2,1,0:T(1,128)}), s32[128,1,12]{2,1,0:T(1,128)S(1)}, u32[]{:S(2)}, u32[]{:S(2)}) async-start(s32[128,1,12]{2,1,0:T(1,128)} %copy.30), calls=%async_computation | async-start | bytes 131072 | tf_op jit(solution)/shard_map/all_to_all | solution.py:44
  30.8 7.3 %scatter_custom_fusion.2 = f32[1536,512]{1,0:T(8,128)} fusion(s32[1024]{0:T(1024)S(1)} %broadcast_select_fusion.1, f32[1024,512]{1,0:T(8,128)} %all-gather.2.cloned.1.call-done, f32[]{:T(128)} %constant.21.clone.1), kind=kCustom, calls=%fused_computation.9 | custom fusion | bytes 3146240
  38.1 5.7 %copy.31 = f32[128,12,512]{2,1,0:T(8,128)} copy(f32[128,12,512]{2,0,1:T(8,128)} %bitcast.55) | data formatting | bytes 6291456 | tf_op jit(solution)/shard_map/scatter | solution.py:34
  43.8 14.3 %all-to-all-start.1 = ((f32[128,12,512]{2,1,0:T(8,128)}), f32[128,12,512]{2,1,0:T(8,128)}, u32[]{:S(2)}, u32[]{:S(2)}) async-start(f32[128,12,512]{2,1,0:T(8,128)} %copy.31), calls=%async_computation.1 | async-start | bytes 8388608 | tf_op jit(solution)/shard_map/all_to_all | solution.py:43
  58.2 2.8 multiply_reduce_fusion.1
  61.3 132.4 %psum.14 = f32[128]{0:T(128)S(1)} all-reduce(f32[128]{0:T(128)S(1)} %select_reduce_fusion), channel_id=1, replica_groups=mesh['dp'=128,'mp'=2] {'dp','mp'}, use_global_device_ids=true, to_apply=%region_9.10 | all-reduce | flops 128 | bytes 1024 | tf_op jit(solution)/shard_map/psum | solution.py:46
  195.6 0.8 reduce.12
  196.7 4.7 %reshape.157 = f32[1536,512]{1,0:T(8,128)} reshape(f32[128,12,512]{2,1,0:T(8,128)} %all-to-all-done.1) | data formatting | bytes 6291456 | tf_op jit(solution)/shard_map/reshape | solution.py:52
  201.4 9.0 %scatter_custom_fusion = f32[1024,512]{1,0:T(8,128)} fusion(s32[1536]{0:T(1024)S(1)} %fusion.21, f32[1536,512]{1,0:T(8,128)} %reshape.157, f32[]{:T(128)} %constant.21.clone.1), kind=kCustom, calls=%fused_computation.22 | custom fusion | bytes 2097664 | tf_op jit(solution)/shard_map/scatter | solution.py:52
  210.3 3.6 %multiply_reduce_fusion = (f32[]{:T(128)}, f32[256,1024]{1,0:T(8,128)S(1)}) fusion(bf16[1,1024,1024]{2,1,0:T(8,128)(2,1)S(1)} %copy-done, f32[1024,512]{1,0:T(8,128)} %scatter_custom_fusion, bf16[1,512,256]{2,1,0:T(8,128)(2,1)S(1)} %copy-done.4), kind=kOutput, calls=%fused_computation.19 | convolution fusion | flops 806617088 | bytes 5505028 | tf_op jit(solution)/shard_map/dot_general | solution.py:76
  214.0 3.1 %psum.15 = f32[]{:T(128)} all-reduce(f32[]{:T(128)} %get-tuple-element.9), channel_id=1, replica_groups=mesh['dp'=128,'mp'=2] {'mp'}, use_global_device_ids=true, to_apply=%region_12.13 | all-reduce | flops 1 | bytes 8 | tf_op jit(solution)/shard_map/psum | solution.py:78
  217.8 0.9 fusion.13
  218.7 1.2 copy.32
  219.9 4.8 %gather_fusion = bf16[1536,256]{1,0:T(8,128)(2,1)S(1)} fusion(bf16[1024,256]{1,0:T(8,128)(2,1)S(1)} %copy.32, s32[2048]{0:T(1024)S(1)} %pad_clamp_fusion), kind=kCustom, calls=%fused_computation | custom fusion | bytes 1579008 | tf_op jit(solution)/shard_map/jit(_take)/gather | solution.py:81
  224.7 1.2 reshape.140
  225.9 2.3 broadcast_select_fusion
  228.2 10.2 %all-to-all-start.2 = ((bf16[128,12,256]{2,1,0:T(8,128)(2,1)}), bf16[128,12,256]{2,1,0:T(8,128)(2,1)}, u32[]{:S(2)}, u32[]{:S(2)}) async-start(bf16[128,12,256]{2,1,0:T(8,128)(2,1)} %broadcast_select_fusion), calls=%async_computation.2 | async-start | bytes 2097152 | tf_op jit(solution)/shard_map/all_to_all | solution.py:82
  238.5 4.8 %fusion.5 = f32[1,256,512]{2,1,0:T(8,128)} fusion(f32[1024,512]{1,0:T(8,128)} %scatter_custom_fusion, s32[]{:T(128)S(6)} %select_n.82, f32[1,256,512]{2,1,0:T(8,128)S(1)} %copy-done.3), kind=kOutput, calls=%fused_computation.14 | convolution fusion | flops 1610874880 | bytes 4194308 | tf_op jit(solution)/shard_map/dot_general | solution.py:65
  243.2 5.9 %fusion = f32[1,512,1024]{2,1,0:T(8,128)} fusion(f32[1,512,1024]{2,1,0:T(8,128)} %param.11, f32[1024,512]{1,0:T(8,128)S(1)} %copy-done.1, s32[]{:T(128)S(6)} %select_n.81), kind=kOutput, calls=%fused_computation.6 | convolution fusion | flops 3222274048 | bytes 7340036 | tf_op jit(solution)/shard_map/dot_general | solution.py:58
  249.2 20.0 %all-to-all-done.2 = bf16[128,12,256]{2,1,0:T(8,128)(2,1)} async-done(((bf16[128,12,256]{2,1,0:T(8,128)(2,1)}), bf16[128,12,256]{2,1,0:T(8,128)(2,1)}, u32[]{:S(2)}, u32[]{:S(2)}) %all-to-all-start.2) | async-done | bytes 786464 | tf_op jit(solution)/shard_map/all_to_all | solution.py:82
  269.2 1.5 copy.33
  270.7 10.5 %gather_fusion.1 = bf16[1024,256]{1,0:T(8,128)(2,1)} fusion(bf16[128,12,256]{2,0,1:T(8,128)(2,1)S(1)} %copy.33, s32[1024]{0:T(1024)S(1)} %bitcast.54), kind=kCustom, calls=%fused_computation.1 | custom fusion | bytes 1056768 | tf_op jit(solution)/shard_map/gather | solution.py:83
  (45 shorter events, 4.3 us)
Async XLA Ops:
  7.2 203.2 %copy-start = (bf16[1,1024,1024]{2,1,0:T(8,128)(2,1)S(1)}, bf16[1,1024,1024]{2,1,0:T(8,128)(2,1)}, u32[]{:S(2)}) copy-start(bf16[1,1024,1024]{2,1,0:T(8,128)(2,1)} %param.13) | copy-start | bytes 6291460
  7.2 2.7 copy-start.8
  7.2 2.8 copy-start.7
  7.2 23.6 %all-gather.2.cloned.1.call-start = ((), (), s32[]{:S(2)}) async-start(), calls=%async_computation.3 | async-start | bytes 3145728 | tf_op jit(solution)/shard_map/all_gather | solution.py:29
  15.3 28.5 %all-to-all-start = ((s32[128,1,12]{2,1,0:T(1,128)}), s32[128,1,12]{2,1,0:T(1,128)S(1)}, u32[]{:S(2)}, u32[]{:S(2)}) async-start(s32[128,1,12]{2,1,0:T(1,128)} %copy.30), calls=%async_computation | async-start | bytes 131072 | tf_op jit(solution)/shard_map/all_to_all | solution.py:44
  43.8 14.4 %copy-start.2 = (f32[1024,256]{1,0:T(8,128)S(1)}, f32[1024,256]{1,0:T(8,128)}, u32[]{:S(2)}) copy-start(f32[1024,256]{1,0:T(8,128)} %param.9) | copy-start | bytes 3145732
  43.8 152.8 %all-to-all-start.1 = ((f32[128,12,512]{2,1,0:T(8,128)}), f32[128,12,512]{2,1,0:T(8,128)}, u32[]{:S(2)}, u32[]{:S(2)}) async-start(f32[128,12,512]{2,1,0:T(8,128)} %copy.31), calls=%async_computation.1 | async-start | bytes 8388608 | tf_op jit(solution)/shard_map/all_to_all | solution.py:43
  58.2 2.8 copy-start.5
  58.2 135.6 %copy-start.6 = (s32[128]{0:T(128)S(1)}, s32[128]{0:T(128)}, u32[]{:S(2)}) copy-start(s32[128]{0:T(128)} %param.17) | copy-start | bytes 1540
  201.4 9.0 %copy-start.4 = (bf16[1,512,256]{2,1,0:T(8,128)(2,1)S(1)}, bf16[1,512,256]{2,1,0:T(8,128)(2,1)}, u32[]{:S(2)}) copy-start(bf16[1,512,256]{2,1,0:T(8,128)(2,1)} %param.14) | copy-start | bytes 786436
  225.9 12.5 %copy-start.3 = (f32[1,256,512]{2,1,0:T(8,128)S(1)}, f32[1,256,512]{2,1,0:T(8,128)}, u32[]{:S(2)}) copy-start(f32[1,256,512]{2,1,0:T(8,128)} %param.12) | copy-start | bytes 1572868
  228.2 41.0 %all-to-all-start.2 = ((bf16[128,12,256]{2,1,0:T(8,128)(2,1)}), bf16[128,12,256]{2,1,0:T(8,128)(2,1)}, u32[]{:S(2)}, u32[]{:S(2)}) async-start(bf16[128,12,256]{2,1,0:T(8,128)(2,1)} %broadcast_select_fusion), calls=%async_computation.2 | async-start | bytes 2097152 | tf_op jit(solution)/shard_map/all_to_all | solution.py:82
  238.4 4.8 %copy-start.1 = (f32[1024,512]{1,0:T(8,128)S(1)}, f32[1024,512]{1,0:T(8,128)}, u32[]{:S(2)}) copy-start(f32[1024,512]{1,0:T(8,128)} %scatter_custom_fusion) | copy-start | bytes 6291460
Sparse Core Ops, SparseCore 0:
  9.8 18.8 all-gather.1
where the time goes:
time: 289 us; the launch traced here: 288 us
  blocking collectives  135 us (47%)
  local copies, waits for them, and re-layouts  52 us (18%)
  starting transfers between devices  40 us (14%)
  waiting for transfers between devices  20.8 us (7%)
  between operations  15.7 us (5%)
  matrix products  14.4 us (5%)
  other arithmetic  9.7 us (3%)
    psum x1, blocking collectives, body(): totals = lax.psum(partial_sums, ('dp', 'mp'))  132 us
    all_to_all x1, waiting for transfers between devices, body(): lax.all_to_all(returning, 'dp', split_axis=0, concat_axis=0, tiled=True)  20 us
    all_to_all x1, starting transfers between devices, body(): lax.all_to_all(send_pos, 'dp', split_axis=0, concat_axis=0, tiled=True)  15.4 us
    all_to_all x1, starting transfers between devices, body(): lax.all_to_all(send_rows, 'dp', split_axis=0, concat_axis=0, tiled=True)  14.3 us
    unnamed x20, local copies, waits for them, and re-layouts  11.8 us
    gather x1, local copies, waits for them, and re-layouts, body(): update = returned[target, slot_index]  10.5 us
    all_to_all x1, starting transfers between devices, body(): lax.all_to_all(returning, 'dp', split_axis=0, concat_axis=0, tiled=True)  10.2 us
    scatter x1, local copies, waits for them, and re-layouts, body(): gathered = jnp.zeros((block_rows, row_width), jnp.float32).at[flat_pos].s...  8.95 us
  transfers between devices with their start and end apart: 4, of which 1 were waited for; matrix products, arithmetic and copies ran while one was open for 13% of the time, Pallas kernels for 0%

commit v1 on v0

v1 whole, which is shorter than its diff:
```python
import functools
import jax
import jax.numpy as jnp
from jax import lax
from jax.experimental import pallas as pl
from jax.experimental.pallas import tpu as pltpu
from jax.sharding import PartitionSpec as P

GRAM_DECAY = 0.95
MOMENT_DECAY = 0.99
ADAM_EPS = 1e-08
GRAFT_EPS = 1e-06

CAP = 12
OUT = CAP + 1
LANES = 128
BF = jnp.bfloat16
F32 = jnp.float32
VMEM_LIMIT = 32 * 1024 * 1024
CHUNKS = 3
VMEM = pl.BlockSpec(memory_space=pltpu.VMEM)
SMEM = pl.BlockSpec(memory_space=pltpu.SMEM)
HBM = pl.BlockSpec(memory_space=pltpu.HBM)
shape = jax.ShapeDtypeStruct


def iota(shape, dim):
    return lax.broadcasted_iota(jnp.int32, shape, dim)


def dot(a, b):
    return jnp.dot(a, b, preferred_element_type=F32)


def dot_nt(a, b):
    return lax.dot_general(a, b, (((1,), (1,)), ((), ())), preferred_element_type=F32)


def onehot(mask):
    return jnp.where(mask, 1.0, 0.0).astype(BF)


def split3(x):
    hi = x.astype(BF)
    rest = x - hi.astype(F32)
    mid = rest.astype(BF)
    lo = (rest - mid.astype(F32)).astype(BF)
    return hi, mid, lo


def keep(x):
    return pltpu.with_memory_space_constraint(x, pltpu.HBM)


def call(kernel, out_shape, in_specs, out_specs=None, scratch=(), flops=0, nbytes=0):
    return pl.pallas_call(
        kernel,
        out_shape=out_shape,
        in_specs=in_specs,
        out_specs=out_specs if out_specs else jax.tree.map(lambda _: VMEM, out_shape),
        scratch_shapes=list(scratch),
        compiler_params=pltpu.CompilerParams(vmem_limit_bytes=VMEM_LIMIT),
        cost_estimate=pl.CostEstimate(flops=flops, bytes_accessed=nbytes, transcendentals=0),
    )


def ranks(dest):
    rows = dest.shape[1]
    step = 256 if rows % 256 == 0 else rows
    before = onehot(iota((step, step), 0) < iota((step, step), 1))
    found, parts = 0.0, []
    for start in range(0, rows, step):
        part = dest[:, start : start + step]
        parts.append(dot(part, before) + found)
        found = found + jnp.sum(part.astype(F32), axis=1, keepdims=True)
    return jnp.concatenate(parts, axis=1)


def pack_kernel(
    n, grad_hbm, moment_hbm, block_hbm, row_hbm, owner_hbm, send_ref, place_ref, new_hbm,
    grad_ref, moment_ref, block_ref, row_ref, owner_ref, scr, sems,
):
    rows = grad_ref.shape[0]
    pairs = (
        (block_hbm, block_ref), (owner_hbm, owner_ref), (row_hbm, row_ref), (grad_hbm, grad_ref),
        (moment_hbm, moment_ref),
    )
    copies = [pltpu.make_async_copy(a, b, sems.at[i]) for i, (a, b) in enumerate(pairs)]
    for copy in copies:
        copy.start()
    for copy in copies[:3]:
        copy.wait()
    block = block_ref[...]
    blocks = onehot(iota((n, rows), 0) == block)
    owner = jnp.broadcast_to(owner_ref[...], (16, n)).astype(F32).astype(BF)
    target = dot(owner, blocks)[0:1].astype(jnp.int32)
    mine = iota((n, rows), 0) == target
    dest = onehot(mine)
    slot = jnp.sum(jnp.where(mine, ranks(dest), 0.0), axis=0, keepdims=True).astype(jnp.int32)
    place_ref[...] = CAP * target + slot
    code = OUT * target + slot
    lane = iota((LANES, rows), 0)
    position = row_ref[...] + 1
    spread = jnp.where(lane == slot, position // 32, 0) + jnp.where(lane == slot + 16, position % 32, 0)
    meta = dot_nt(dest, spread.astype(F32).astype(BF))
    copies[3].wait()
    copies[4].wait()

    grad = grad_ref[...]
    square = grad * grad
    moment = MOMENT_DECAY * moment_ref[...] + (1.0 - MOMENT_DECAY) * square
    moment_ref[...] = moment
    store = pltpu.make_async_copy(moment_ref, new_hbm, sems.at[5])
    store.start()
    denom = jnp.sqrt(moment) + ADAM_EPS
    step = grad / denom
    step_sq = step * step
    half = step_sq[:, :LANES] + step_sq[:, LANES:]
    hi, mid, lo = split3(half)
    adam = jnp.sum(dot(dest, hi) + dot(dest, mid) + dot(dest, lo), axis=1, keepdims=True)
    a_hi, a_mid, a_lo = split3(adam)
    col = iota((n, LANES), 1)
    meta = jnp.where(col == 32, a_hi.astype(F32), meta)
    meta = jnp.where(col == 33, a_mid.astype(F32), meta)
    meta = jnp.where(col == 34, a_lo.astype(F32), meta)

    placed = dot(onehot(iota((OUT * n, rows), 0) == code), grad.astype(BF))
    scr[pl.ds(0, OUT * n, stride=2), :] = placed[:, :LANES]
    scr[pl.ds(1, OUT * n, stride=2), :] = placed[:, LANES:]
    scr[pl.ds(2 * CAP, n, stride=2 * OUT), :] = meta
    send_ref[...] = scr[...].astype(BF)
    store.wait()


def pack(n, gradient, moment, block, row, owner):
    rows, width = gradient.shape
    return call(
        functools.partial(pack_kernel, n),
        (shape((2 * OUT * n, LANES), BF), shape((1, rows), jnp.int32), shape((rows, width), F32)),
        [HBM] * 5,
        (VMEM, VMEM, HBM),
        [
            pltpu.VMEM((rows, width), F32),
            pltpu.VMEM((rows, width), F32),
            pltpu.VMEM((1, rows), jnp.int32),
            pltpu.VMEM((1, rows), jnp.int32),
            pltpu.VMEM((1, n), jnp.int32),
            pltpu.VMEM((2 * OUT * n, LANES), F32),
            pltpu.SemaphoreType.DMA((6,)),
        ],
        flops=2 * OUT * n * rows * width, nbytes=4 * 2**20,
    )(*[keep(x) for x in (gradient, moment, block, row, owner)])


def column_halves(scr, start, slots):
    left = scr[pl.ds(2 * start, slots, stride=2), :].astype(BF)
    right = scr[pl.ds(2 * start + 1, slots, stride=2), :].astype(BF)
    return jnp.concatenate([left, right], axis=1)


def tile_kernel(n, got_ref, left_hbm, tile_ref, adam_ref, meta_ref, left_ref, scr, sem):
    load = pltpu.make_async_copy(left_hbm.at[pl.ds(0, left_ref.shape[0])], left_ref, sem)
    load.start()
    rows = tile_ref.shape[0]
    scr[...] = got_ref[...].astype(F32)
    meta = scr[pl.ds(2 * CAP, n, stride=2 * OUT), :]
    meta_ref[...] = meta
    col = iota((n, LANES), 1)
    adam = jnp.sum(jnp.where((col >= 32) & (col < 35), meta, 0.0), axis=(0, 1), keepdims=True)
    adam_ref[...] = jnp.broadcast_to(adam, adam_ref.shape)
    source = iota((n, OUT * n), 0)
    slots = iota((n, OUT * n), 1)
    expand = onehot((slots >= OUT * source) & (slots < OUT * source + OUT))
    by_slot = dot(meta.T.astype(BF), expand)
    position = 32.0 * by_slot[0:16] + by_slot[16:32]
    which = iota((16, OUT * n), 1) % OUT
    position = jnp.sum(
        jnp.where(iota((16, OUT * n), 0) == which, position, 0.0), axis=0, keepdims=True
    ).astype(jnp.int32)
    order = onehot(iota((rows, OUT * n), 0) + 1 == position)
    tile_ref[...] = dot(order, column_halves(scr, 0, OUT * n)).astype(BF)
    load.wait()


def tile(n, rows, got, left):
    return call(
        functools.partial(tile_kernel, n),
        (
            shape((rows, 2 * LANES), BF), shape((8, LANES), F32), shape((n, LANES), F32),
            shape((rows // 2, rows), BF),
        ),
        [VMEM, HBM],
        scratch=[pltpu.VMEM((2 * OUT * n, LANES), F32), pltpu.SemaphoreType.DMA],
        flops=2 * OUT * n * rows * 2 * LANES, nbytes=3 * 2**20,
    )(got, keep(left))


def return_order_kernel(n, meta_ref, left_hbm, order_ref, left_ref, sem):
    half = left_ref.shape[0]
    load = pltpu.make_async_copy(left_hbm.at[pl.ds(half, half)], left_ref, sem)
    load.start()
    rows = order_ref.shape[1]
    slots = iota((CAP * n, n), 0)
    source = iota((CAP * n, n), 1)
    expand = onehot((slots >= CAP * source) & (slots < CAP * source + CAP))
    meta = meta_ref[...]
    meta = jnp.where(iota((n, LANES), 1) < 16, 32.0 * meta, meta).astype(BF)
    by_slot = dot(expand, meta)
    which = iota((CAP * n, LANES), 0) % CAP
    lane = iota((CAP * n, LANES), 1)
    chosen = jnp.where((lane == which) | (lane == which + 16), by_slot, 0.0).astype(BF)
    position = dot(chosen, jnp.ones((LANES, LANES), BF)).astype(jnp.int32)
    lane = lane + 1
    for j in range(0, rows, LANES):
        order_ref[:, j : j + LANES] = onehot(position == lane + j)
    load.wait()


def return_order(n, rows, meta, left):
    return call(
        functools.partial(return_order_kernel, n),
        (shape((CAP * n, rows), BF), shape((rows // 2, rows), BF)),
        [VMEM, HBM],
        scratch=[pltpu.SemaphoreType.DMA],
        flops=4 * CAP * n * n * LANES, nbytes=4 * 2**20,
    )(meta, keep(left))


def precond_kernel(
    n, core_ref, own_ref, other_ref, adam_own_ref, adam_other_ref, order_ref, root_own_ref,
    root_other_ref, left_top_ref, left_bottom_ref, back_hbm, scr, back_ref, sems,
):
    rows, width = own_ref.shape
    core = core_ref[0]
    own_rows = pl.ds(pl.multiple_of(core * width, width), width)
    other_rows = pl.ds(pl.multiple_of((1 - core) * width, width), width)
    own, other = own_ref[...], other_ref[...]
    mixed_own = dot(own, root_own_ref[own_rows, :]) + dot(other, root_own_ref[other_rows, :])
    mixed_other = dot(own, root_other_ref[own_rows, :]) + dot(other, root_other_ref[other_rows, :])
    mixed_own, mixed_other = mixed_own.astype(BF), mixed_other.astype(BF)
    parts, total = [], 0.0
    for left_ref in (left_top_ref, left_bottom_ref):
        for start in range(0, rows // 2, rows // 4):
            left = left_ref[start : start + rows // 4, :]
            part, other_part = dot(left, mixed_own), dot(left, mixed_other)
            squares = part * part + other_part * other_part
            total = total + jnp.sum(squares.reshape(rows // 32, 8, width), axis=0)
            parts.append(part)
    total = jnp.sum(total, axis=(0, 1), keepdims=True)
    adam = adam_own_ref[0:1, 0:1] + adam_other_ref[0:1, 0:1]
    scale = jnp.sqrt(adam) / (jnp.sqrt(total) + GRAFT_EPS)
    grafted = jnp.concatenate([(part * scale).astype(BF) for part in parts], axis=0)
    part = CAP * n // CHUNKS
    stores = []
    for i in range(CHUNKS):
        chunk = pl.ds(2 * part * i, 2 * part)
        placed = dot(order_ref[part * i : part * (i + 1), :], grafted)
        scr[pl.ds(2 * part * i, part, stride=2), :] = placed[:, :LANES]
        scr[pl.ds(2 * part * i + 1, part, stride=2), :] = placed[:, LANES:]
        back_ref[chunk, :] = scr[chunk, :].astype(BF)
        store = pltpu.make_async_copy(back_ref.at[chunk], back_hbm.at[chunk], sems.at[i])
        store.start()
        stores.append(store)
    for store in stores:
        store.wait()


def precond(
    n, core, own, other, adam_own, adam_other, order, root_own, root_other, left_top, left_bottom
):
    rows, width = own.shape
    return call(
        functools.partial(precond_kernel, n),
        shape((2 * CAP * n, LANES), BF),
        [SMEM] + [VMEM] * 9,
        HBM,
        scratch=[
            pltpu.VMEM((2 * CAP * n, LANES), F32),
            pltpu.VMEM((2 * CAP * n, LANES), BF),
            pltpu.SemaphoreType.DMA((CHUNKS,)),
        ],
        flops=8 * rows * rows * width, nbytes=5 * 2**20,
    )(core, own, other, adam_own, adam_other, order, root_own, root_other, left_top, left_bottom)


def flat_order_kernel(n, place_ref, after_ref, order_ref):
    del after_ref
    rows = order_ref.shape[0]
    place = jnp.broadcast_to(place_ref[...].astype(F32), (LANES, rows)).T.astype(jnp.int32)
    lane = iota((rows, LANES), 1)
    for j in range(0, CAP * n, LANES):
        order_ref[:, j : j + LANES] = onehot(place == lane + j)


def flat_order(n, place, after):
    rows = place.shape[1]
    return call(
        functools.partial(flat_order_kernel, n),
        shape((rows, CAP * n), BF),
        [VMEM, pl.BlockSpec(memory_space=pl.ANY)],
        flops=0, nbytes=3 * 2**20,
    )(place, after)


def unpack_kernel(n, back_hbm, order_ref, update_hbm, back_ref, scr, update_ref, sems):
    rows = update_ref.shape[0]
    part = CAP * n // CHUNKS
    loads = []
    for i in range(CHUNKS):
        chunk = pl.ds(2 * part * i, 2 * part)
        loads.append(pltpu.make_async_copy(back_hbm.at[chunk], back_ref.at[chunk], sems.at[i]))
        loads[i].start()
    halves = [pl.ds(i * (rows // 2), rows // 2) for i in range(2)]
    sums = [0.0, 0.0]
    for i in range(CHUNKS):
        chunk = pl.ds(2 * part * i, 2 * part)
        loads[i].wait()
        scr[chunk, :] = back_ref[chunk, :].astype(F32)
        came = column_halves(scr, part * i, part)
        for j, half in enumerate(halves):
            sums[j] = sums[j] + dot(order_ref[half, part * i : part * (i + 1)], came)
            if i == CHUNKS - 1:
                update_ref[half, :] = sums[j].astype(BF)
                store = pltpu.make_async_copy(update_ref.at[half], update_hbm.at[half], sems.at[CHUNKS + j])
                store.start()
                loads.append(store)
    for store in loads[CHUNKS:]:
        store.wait()


def unpack(n, back, order):
    rows = order.shape[0]
    return call(
        functools.partial(unpack_kernel, n),
        shape((rows, 2 * LANES), BF),
        [HBM, VMEM],
        HBM,
        scratch=[
            pltpu.VMEM((2 * CAP * n, LANES), BF),
            pltpu.VMEM((2 * CAP * n, LANES), F32),
            pltpu.VMEM((rows, 2 * LANES), BF),
            pltpu.SemaphoreType.DMA((CHUNKS + 2,)),
        ],
        flops=2 * CAP * n * rows * 2 * LANES, nbytes=2 * 2**20,
    )(back, order)


def body(
    gradient, moment, left_stat, right_stat, left_root, right_root, seg_block, seg_row, owner_table
):
    n = lax.axis_size("dp")
    rows = gradient.shape[0]
    core = lax.axis_index("mp").astype(jnp.int32)
    swap = [(0, 1), (1, 0)]
    root_own = right_root[0]
    root_other = lax.ppermute(root_own, "mp", swap)

    send, place, moment_new = pack(
        n, gradient, moment, seg_block[None, :], seg_row[None, :], owner_table[None, :]
    )
    send, root_other = lax.optimization_barrier((send, root_other))
    got = lax.all_to_all(send.reshape(n, OUT, 2, LANES), "dp", 0, 0, tiled=True)
    got = got.reshape(2 * OUT * n, LANES)
    tile_own, adam_own, meta, left_top = tile(n, rows, got, left_root[0])
    tile_other = lax.ppermute(tile_own, "mp", swap)
    adam_other = lax.ppermute(adam_own, "mp", swap)
    order, left_bottom = return_order(n, rows, meta, left_root[0])
    back = precond(
        n, core[None], tile_own, tile_other, adam_own, adam_other, order, root_own, root_other,
        left_top, left_bottom,
    )
    returned = lax.all_to_all(back.reshape(n, 2 * CAP, LANES), "dp", 0, 0, tiled=True)

    order = flat_order(n, place, back)
    whole = jnp.where(
        core == 0,
        jnp.concatenate([tile_own, tile_other], axis=1),
        jnp.concatenate([tile_other, tile_own], axis=1),
    )
    stat_rows = left_stat.shape[1]
    own_rows = lax.dynamic_slice_in_dim(whole, core * stat_rows, stat_rows, 0)
    left_new = GRAM_DECAY * left_stat[0] + dot_nt(own_rows, whole)
    right_new = GRAM_DECAY * right_stat[0] + lax.dot_general(
        tile_own, whole, (((0,), (0,)), ((), ())), preferred_element_type=F32
    )
    update = unpack(n, returned.reshape(2 * CAP * n, LANES), order)
    return (update, moment_new, left_new[None], right_new[None])


def solution(mesh):
    in_specs = (
        P("dp", "mp"),
        P("dp", "mp"),
        P("dp", "mp", None),
        P("dp", "mp", None),
        P("dp", None, None),
        P("dp", None, "mp"),
        P("dp"),
        P("dp"),
        P(),
    )
    out_specs = (P("dp", "mp"), P("dp", "mp"), P("dp", "mp", None), P("dp", "mp", None))
    return jax.shard_map(body, mesh=mesh, in_specs=in_specs, out_specs=out_specs, check_vma=False)
```

time: 289 us -> 92.2 us (0.32)
  blocking collectives: 135 us -> 42.8 us
  local copies, waits for them, and re-layouts: 52 us -> 0.52 us
  starting transfers between devices: 40 us -> 8.36 us
  between operations: 15.7 us -> 0.97 us
  Pallas kernels: 0 us -> 14.6 us
  matrix products: 14.4 us -> 3.34 us
  other arithmetic: 9.7 us -> 1.81 us
    psum x2 -> x0, blocking collectives: 135 us -> none  [the longest x1 132 us: body(): totals = lax.psum(partial_sums, ('dp', 'mp'))]
    all_to_all x0 -> x1, blocking collectives: none -> 42.8 us  [body(): got = lax.all_to_all(send.reshape(n, OUT, 2, LANES), 'dp', 0, 0, tiled=True)]
    all_to_all x3 -> x1, starting transfers between devices: 39.9 us -> 7.68 us  [body(): lax.all_to_all(back.reshape(n, 2 * CAP, LANES), 'dp', 0, 0, tiled=True)]
    gather x3 -> x0, local copies, waits for them, and re-layouts: 16.5 us -> none  [the longest x1 10.5 us: body(): update = returned[target, slot_index]]
    scatter x2 -> x0, local copies, waits for them, and re-layouts: 14.7 us -> none  [the longest x1 8.95 us: body(): gathered = jnp.zeros((block_rows, row_width), jnp.float32).at[flat_pos].s...]
    pallas_call x0 -> x6, Pallas kernels: none -> 14.6 us  [the longest x1 4.41 us: precond(): call(functools.partial(precond_kernel, n), shape((2 * CAP * n, LANES), BF...]
    unnamed x20 -> x14, local copies, waits for them, and re-layouts: 11.8 us -> 0.52 us
    dot_general x3 -> x2, matrix products: 14.4 us -> 3.34 us  [the longest x1 2.06 us: dot_nt(): lax.dot_general(a, b, (((1,), (1,)), ((), ())), preferred_element_type=F32)]
  transfers between devices with their start and end apart: 4 -> 4, of which waited for: 1 -> 2; matrix products, arithmetic and copies ran while one was open for 13% -> 6% of each run, Pallas kernels for 0% -> 6%
where the time goes in v1:
time: 92.2 us; the launch traced here: 91.9 us
  blocking collectives  42.8 us (46%)
  waiting for transfers between devices  19.6 us (21%)
  Pallas kernels  14.6 us (16%)
  starting transfers between devices  8.36 us (9%)
  matrix products  3.34 us (4%)
  other arithmetic  1.81 us (2%)
  between operations  0.97 us (1%)
    all_to_all x1, blocking collectives, body(): got = lax.all_to_all(send.reshape(n, OUT, 2, LANES), 'dp', 0, 0, tiled=True)  42.8 us
    all_to_all x1, waiting for transfers between devices, body(): lax.all_to_all(back.reshape(n, 2 * CAP, LANES), 'dp', 0, 0, tiled=True)  19.4 us
    all_to_all x1, starting transfers between devices, body(): lax.all_to_all(back.reshape(n, 2 * CAP, LANES), 'dp', 0, 0, tiled=True)  7.68 us
    pallas_call x1, Pallas kernels, precond(): call(functools.partial(precond_kernel, n), shape((2 * CAP * n, LANES), BF...  4.41 us
    pallas_call x1, Pallas kernels, pack(): call(functools.partial(pack_kernel, n), (shape((2 * OUT * n, LANES), BF),...  3.65 us
    pallas_call x1, Pallas kernels, unpack(): call(functools.partial(unpack_kernel, n), shape((rows, 2 * LANES), BF), [...  2.99 us
    dot_general x1, matrix products, dot_nt(): lax.dot_general(a, b, (((1,), (1,)), ((), ())), preferred_element_type=F32)  2.06 us
  transfers between devices with their start and end apart: 4, of which 2 were waited for; matrix products, arithmetic and copies ran while one was open for 6% of the time, Pallas kernels for 6%

profile of v1, /device:TPU:2, one launch (start us, length us, event | category | flops | bytes accessed | tf_op | source)
XLA Modules:
  0.0 91.9 jit_solution(18430506983919864471)
XLA Ops:
  0.6 0.1 collective-permute-start
  0.7 3.6 %shard_map.120 = (bf16[3328,128]{1,0:T(8,128)(2,1)S(1)}, s32[1,1024]{1,0:T(1,128)S(1)}, f32[1024,256]{1,0:T(8,128)}) custom-call(f32[1024,256]{1,0:T(8,128)} %grad_hbm.1, f32[1024,256]{1,0:T(8,128)} %moment_hbm.1, s32[1,1024]{1,0:T(1,128)} %bitcast.28, s32[1,1024]{1,0:T(1,128)} %bitcast.29, s32[1,128]{1,0:T(1,128)} %bitcast.30), custom_call_target="tpu_custom_call" | custom-call | flops 872415232 | bytes 4194304 | tf_op jit(solution)/shard_map/pallas_call | solution.py:137
  4.4 0.0 collective-permute-done.root_other_ref
  4.4 42.8 %all_to_all.10 = bf16[128,13,2,128]{3,2,1,0:T(2,128)(2,1)S(1)} all-to-all(bf16[128,13,2,128]{3,2,1,0:T(2,128)(2,1)S(1)} %bitcast.22), channel_id=1, replica_groups=mesh['dp'=128,'mp'=2] {'dp'}, dimensions={0} | all-to-all | bytes 1703936 | tf_op jit(solution)/shard_map/all_to_all | solution.py:362
  47.2 1.5 %shard_map.121 = (bf16[1024,256]{1,0:T(8,128)(2,1)S(1)}, f32[8,128]{1,0:T(8,128)S(1)}, f32[128,128]{1,0:T(8,128)S(1)}, bf16[512,1024]{1,0:T(8,128)(2,1)S(1)}) custom-call(bf16[3328,128]{1,0:T(8,128)(2,1)S(1)} %bitcast.23, bf16[1024,1024]{1,0:T(8,128)(2,1)} %bitcast.26), custom_call_target="tpu_custom_call" | custom-call | flops 872415232 | bytes 3145728 | tf_op jit(solution)/shard_map/pallas_call | solution.py:186
  48.7 0.0 copy-start
  48.7 0.1 collective-permute-start.1
  48.9 0.5 collective-permute-start.2
  49.3 1.3 %shard_map.122 = (bf16[1536,1024]{1,0:T(8,128)(2,1)S(1)}, bf16[512,1024]{1,0:T(8,128)(2,1)S(1)}) custom-call(f32[128,128]{1,0:T(8,128)S(1)} %get-tuple-element.19.meta_ref, bf16[1024,1024]{1,0:T(8,128)(2,1)} %bitcast.27), custom_call_target="tpu_custom_call" | custom-call | flops 100663296 | bytes 4194304 | tf_op jit(solution)/shard_map/pallas_call | solution.py:220
  50.6 0.1 collective-permute-done.2.adam_other_ref
  50.7 0.0 collective-permute-done.1.other_ref
  50.8 4.4 %shard_map.123.after_ref = bf16[3072,128]{1,0:T(8,128)(2,1)} custom-call(s32[1]{0:T(128)} %bitcast.core_ref, bf16[1024,256]{1,0:T(8,128)(2,1)S(1)} %get-tuple-element.17.own_ref, bf16[1024,256]{1,0:T(8,128)(2,1)S(1)} %collective-permute-done.1.other_ref, f32[8,128]{1,0:T(8,128)S(1)} %get-tuple-element.18.adam_own_ref, ...), custom_call_target="tpu_custom_call" | custom-call | flops 2147483648 | bytes 5242880 | tf_op jit(solution)/shard_map/pallas_call | solution.py:272
  55.2 7.7 %all-to-all-start.1 = ((bf16[128,24,128]{2,1,0:T(8,128)(2,1)}), bf16[128,24,128]{2,1,0:T(8,128)(2,1)}, u32[]{:S(2)}, u32[]{:S(2)}) async-start(bf16[128,24,128]{2,1,0:T(8,128)(2,1)} %bitcast.8), calls=%async_computation.1 | async-start | bytes 1572864 | tf_op jit(solution)/shard_map/all_to_all | solution.py:372
  62.9 0.0 copy-start.1
  62.9 0.0 copy-start.3
  62.9 0.0 copy-start.6
  62.9 0.7 shard_map.124.order_ref
  63.6 1.8 %maximum_select_fusion = bf16[1024,512]{1,0:T(8,128)(2,1)S(1)} fusion(bf16[1024,256]{1,0:T(8,128)(2,1)} %copy-done.2, bf16[1024,256]{1,0:T(8,128)(2,1)} %copy-done, pred[]{:T(512)S(6)} %eq.3), kind=kLoop, calls=%fused_computation.4 | loop fusion | flops 4718592 | bytes 2097153 | tf_op jit(solution)/shard_map/jit(_where)/select_n | solution.py:375
  65.5 0.0 copy-start.5
  65.5 1.3 %fusion.1 = f32[1,256,512]{2,1,0:T(8,128)} fusion(bf16[1024,256]{1,0:T(8,128)(2,1)S(1)} %copy-done.1, f32[1,256,512]{2,1,0:T(8,128)S(1)} %copy-done.6, bf16[1024,256]{1,0:T(8,128)(2,1)S(1)} %copy-done.3, pred[]{:T(512)S(6)} %eq.3), kind=kOutput, calls=%fused_computation.3 | convolution fusion | flops 273416192 | bytes 2097153 | tf_op jit(solution)/shard_map/dot_general | solution.py:383
  66.8 0.5 copy-done.5
  67.3 2.1 %fusion = f32[1,512,1024]{2,1,0:T(8,128)} fusion(f32[1,512,1024]{2,1,0:T(8,128)S(1)} %copy-done.5, bf16[1024,512]{1,0:T(8,128)(2,1)S(1)} %maximum_select_fusion, s32[]{:T(128)S(6)} %select_n.13), kind=kOutput, calls=%fused_computation.1 | convolution fusion | flops 537919488 | bytes 5767172 | tf_op jit(solution)/shard_map/dot_general | solution.py:36
  69.3 19.4 %all-to-all-done.1 = bf16[128,24,128]{2,1,0:T(8,128)(2,1)} async-done(((bf16[128,24,128]{2,1,0:T(8,128)(2,1)}), bf16[128,24,128]{2,1,0:T(8,128)(2,1)}, u32[]{:S(2)}, u32[]{:S(2)}) %all-to-all-start.1) | async-done | bytes 786464 | tf_op jit(solution)/shard_map/all_to_all | solution.py:372
  88.8 3.0 %shard_map.125 = bf16[1024,256]{1,0:T(8,128)(2,1)} custom-call(bf16[3072,128]{1,0:T(8,128)(2,1)} %bitcast.9.back_hbm, bf16[1024,1536]{1,0:T(8,128)(2,1)S(1)} %shard_map.124.order_ref), custom_call_target="tpu_custom_call" | custom-call | flops 805306368 | bytes 2097152 | tf_op jit(solution)/shard_map/pallas_call | solution.py:333
  (8 shorter events, 0.0 us)
Async XLA Ops:
  0.6 3.8 %collective-permute-start = (bf16[512,256]{1,0:T(8,128)(2,1)}, bf16[512,256]{1,0:T(8,128)(2,1)S(1)}, u32[]{:S(2)}, u32[]{:S(2)}) collective-permute-start(bf16[512,256]{1,0:T(8,128)(2,1)} %bitcast.24), channel_id=1, source_target_pairs={{0,1},{1,0},{2,3},{3,2},{4,5},{5,4},{6,7},{7,6},{8,9},{9,8},{10,11... | collective-permute-start | bytes 786440 | tf_op jit(solution)/shard_map/ppermute | solution.py:356
  47.2 3.6 %copy-start.4 = (bf16[1,512,256]{2,1,0:T(8,128)(2,1)S(1)}, bf16[1,512,256]{2,1,0:T(8,128)(2,1)}, u32[]{:S(2)}) copy-start(bf16[1,512,256]{2,1,0:T(8,128)(2,1)} %param.14) | copy-start | bytes 786436
  48.7 6.5 %copy-start = (bf16[1024,256]{1,0:T(8,128)(2,1)}, bf16[1024,256]{1,0:T(8,128)(2,1)S(1)}, u32[]{:S(2)}) copy-start(bf16[1024,256]{1,0:T(8,128)(2,1)S(1)} %get-tuple-element.17.own_ref) | copy-start | bytes 1572868
  48.7 2.0 %collective-permute-start.1 = (bf16[1024,256]{1,0:T(8,128)(2,1)S(1)}, bf16[1024,256]{1,0:T(8,128)(2,1)S(1)}, u32[]{:S(2)}, u32[]{:S(2)}) collective-permute-start(bf16[1024,256]{1,0:T(8,128)(2,1)S(1)} %get-tuple-element.17.own_ref), channel_id=1, source_target_pairs={{0,1},{1,0},{2,3},{3,2},{4,5},{5,4},{6,7},{7,6},{8,9},{9,8},{10,11... | collective-permute-start | bytes 1572872 | tf_op jit(solution)/shard_map/ppermute | solution.py:365
  48.9 1.9 %collective-permute-start.2 = (f32[8,128]{1,0:T(8,128)S(1)}, f32[8,128]{1,0:T(8,128)S(1)}, u32[]{:S(2)}, u32[]{:S(2)}) collective-permute-start(f32[8,128]{1,0:T(8,128)S(1)} %get-tuple-element.18.adam_own_ref), channel_id=1, source_target_pairs={{0,1},{1,0},{2,3},{3,2},{4,5},{5,4},{6,7},{7,6},{8,9},{9,8},{10,11... | collective-permute-start | bytes 12296 | tf_op jit(solution)/shard_map/ppermute | solution.py:366
  50.8 4.4 %copy-start.2 = (bf16[1024,256]{1,0:T(8,128)(2,1)}, bf16[1024,256]{1,0:T(8,128)(2,1)S(1)}, u32[]{:S(2)}) copy-start(bf16[1024,256]{1,0:T(8,128)(2,1)S(1)} %collective-permute-done.1.other_ref) | copy-start | bytes 1572868
  55.2 33.6 %all-to-all-start.1 = ((bf16[128,24,128]{2,1,0:T(8,128)(2,1)}), bf16[128,24,128]{2,1,0:T(8,128)(2,1)}, u32[]{:S(2)}, u32[]{:S(2)}) async-start(bf16[128,24,128]{2,1,0:T(8,128)(2,1)} %bitcast.8), calls=%async_computation.1 | async-start | bytes 1572864 | tf_op jit(solution)/shard_map/all_to_all | solution.py:372
  62.9 2.6 %copy-start.1 = (bf16[1024,256]{1,0:T(8,128)(2,1)S(1)}, bf16[1024,256]{1,0:T(8,128)(2,1)}, u32[]{:S(2)}) copy-start(bf16[1024,256]{1,0:T(8,128)(2,1)} %copy-done) | copy-start | bytes 1572868
  62.9 2.6 %copy-start.3 = (bf16[1024,256]{1,0:T(8,128)(2,1)S(1)}, bf16[1024,256]{1,0:T(8,128)(2,1)}, u32[]{:S(2)}) copy-start(bf16[1024,256]{1,0:T(8,128)(2,1)} %copy-done.2) | copy-start | bytes 1572868
  62.9 2.6 %copy-start.6 = (f32[1,256,512]{2,1,0:T(8,128)S(1)}, f32[1,256,512]{2,1,0:T(8,128)}, u32[]{:S(2)}) copy-start(f32[1,256,512]{2,1,0:T(8,128)} %param.12) | copy-start | bytes 1572868
  65.5 1.8 %copy-start.5 = (f32[1,512,1024]{2,1,0:T(8,128)S(1)}, f32[1,512,1024]{2,1,0:T(8,128)}, u32[]{:S(2)}) copy-start(f32[1,512,1024]{2,1,0:T(8,128)} %param.11) | copy-start | bytes 6291460

commit v2 on v1

v2 whole, which is shorter than its diff:
```python
import functools
import jax
import jax.numpy as jnp
from jax import lax
from jax.experimental import pallas as pl
from jax.experimental.pallas import tpu as pltpu
from jax.sharding import PartitionSpec as P

GRAM_DECAY = 0.95
MOMENT_DECAY = 0.99
ADAM_EPS = 1e-08
GRAFT_EPS = 1e-06

CAP = 12
OUT = CAP + 1
LANES = 128
BF = jnp.bfloat16
F32 = jnp.float32
VMEM_LIMIT = 32 * 1024 * 1024
EXTRA = 16
GROUP = 4
LOADS = 2
CHUNKS = 4
PARTS = 3
VMEM = pl.BlockSpec(memory_space=pltpu.VMEM)
SMEM = pl.BlockSpec(memory_space=pltpu.SMEM)
HBM = pl.BlockSpec(memory_space=pltpu.HBM)
shape = jax.ShapeDtypeStruct


def iota(shape, dim):
    return lax.broadcasted_iota(jnp.int32, shape, dim)


def dot(a, b):
    return jnp.dot(a, b, preferred_element_type=F32)


def dot_nt(a, b):
    return lax.dot_general(a, b, (((1,), (1,)), ((), ())), preferred_element_type=F32)


def onehot(mask):
    return jnp.where(mask, 1.0, 0.0).astype(BF)


def split3(x):
    hi = x.astype(BF)
    rest = x - hi.astype(F32)
    mid = rest.astype(BF)
    lo = (rest - mid.astype(F32)).astype(BF)
    return hi, mid, lo


def keep(x):
    return pltpu.with_memory_space_constraint(x, pltpu.HBM)


def call(kernel, out_shape, in_specs, out_specs=None, scratch=(), flops=0, nbytes=0):
    return pl.pallas_call(
        kernel,
        out_shape=out_shape,
        in_specs=in_specs,
        out_specs=out_specs if out_specs else jax.tree.map(lambda _: VMEM, out_shape),
        scratch_shapes=list(scratch),
        compiler_params=pltpu.CompilerParams(vmem_limit_bytes=VMEM_LIMIT),
        cost_estimate=pl.CostEstimate(flops=flops, bytes_accessed=nbytes, transcendentals=0),
    )


def ranks(dest):
    rows = dest.shape[1]
    step = 256 if rows % 256 == 0 else rows
    before = onehot(iota((step, step), 0) < iota((step, step), 1))
    found, parts = 0.0, []
    for start in range(0, rows, step):
        part = dest[:, start : start + step]
        parts.append(dot(part, before) + found)
        found = found + jnp.sum(part.astype(F32), axis=1, keepdims=True)
    return jnp.concatenate(parts, axis=1)


def next_moment(grad, moment):
    return MOMENT_DECAY * moment + (1.0 - MOMENT_DECAY) * (grad * grad)


def pack_kernel(
    n, grad_hbm, moment_hbm, block_hbm, row_hbm, owner_hbm, send_ref, place_ref, grad_ref,
    moment_ref, block_ref, row_ref, owner_ref, scr, sems,
):
    rows = grad_ref.shape[0]
    pairs = ((block_hbm, block_ref), (owner_hbm, owner_ref), (row_hbm, row_ref))
    copies = [pltpu.make_async_copy(a, b, sems.at[i]) for i, (a, b) in enumerate(pairs)]
    parts = [pl.ds(i * (rows // LOADS), rows // LOADS) for i in range(LOADS)]
    loads = [
        [
            pltpu.make_async_copy(grad_hbm.at[part], grad_ref.at[part], sems.at[3 + 2 * i]),
            pltpu.make_async_copy(moment_hbm.at[part], moment_ref.at[part], sems.at[4 + 2 * i]),
        ]
        for i, part in enumerate(parts)
    ]
    for copy in copies + sum(loads, []):
        copy.start()
    for copy in copies:
        copy.wait()
    block = block_ref[...]
    blocks = onehot(iota((n, rows), 0) == block)
    owner = jnp.broadcast_to(owner_ref[...], (16, n)).astype(F32).astype(BF)
    target = dot(owner, blocks)[0:1].astype(jnp.int32)
    mine = iota((n, rows), 0) == target
    dest = onehot(mine)
    slot = jnp.sum(jnp.where(mine, ranks(dest), 0.0), axis=0, keepdims=True).astype(jnp.int32)
    place_ref[...] = CAP * target + slot
    lane = iota((LANES, rows), 0)
    position = row_ref[...] + 1
    spread = jnp.where(lane == slot, position // 32, 0) + jnp.where(lane == slot + 16, position % 32, 0)
    meta = dot_nt(dest, spread.astype(F32).astype(BF))
    squares, coarse = [], []
    for part, (load_grad, load_moment) in zip(parts, loads):
        load_grad.wait()
        load_moment.wait()
        grad = grad_ref[part, :]
        coarse.append(grad.astype(BF))
        step = grad / (jnp.sqrt(next_moment(grad, moment_ref[part, :])) + ADAM_EPS)
        step_sq = step * step
        half = step_sq[:, :LANES] + step_sq[:, LANES:]
        squares.append(jnp.concatenate(split3(half), axis=1))
    coarse = jnp.concatenate(coarse, axis=0)
    for start in range(0, CAP, GROUP):
        slots = range(start, start + GROUP)
        order = jnp.concatenate([dest * onehot(slot == k) for k in slots], axis=0)
        placed = dot(order, coarse)
        for i, k in enumerate(slots):
            scr[pl.ds(2 * k, n, stride=2 * OUT), :] = placed[n * i : n * (i + 1), :LANES]
            scr[pl.ds(2 * k + 1, n, stride=2 * OUT), :] = placed[n * i : n * (i + 1), LANES:]
    adam = dot(dest, jnp.concatenate(squares, axis=0))
    a_hi, a_mid, a_lo = split3(jnp.sum(adam, axis=1, keepdims=True))
    col = iota((n, LANES), 1)
    meta = jnp.where(col == 32, a_hi.astype(F32), meta)
    meta = jnp.where(col == 33, a_mid.astype(F32), meta)
    meta = jnp.where(col == 34, a_lo.astype(F32), meta)
    scr[pl.ds(2 * CAP, n, stride=2 * OUT), :] = meta
    scr[pl.ds(2 * CAP + 1, n, stride=2 * OUT), :] = jnp.zeros((n, LANES), F32)
    send_ref[...] = scr[...].astype(BF)


def pack(n, gradient, moment, block, row, owner):
    rows, width = gradient.shape
    return call(
        functools.partial(pack_kernel, n),
        (shape((2 * OUT * n, LANES), BF), shape((1, rows), jnp.int32)),
        [HBM] * 5,
        scratch=[
            pltpu.VMEM((rows, width), F32),
            pltpu.VMEM((rows, width), F32),
            pltpu.VMEM((1, rows), jnp.int32),
            pltpu.VMEM((1, rows), jnp.int32),
            pltpu.VMEM((1, n), jnp.int32),
            pltpu.VMEM((2 * OUT * n, LANES), F32),
            pltpu.SemaphoreType.DMA((3 + 2 * LOADS,)),
        ],
        flops=2 * OUT * n * rows * width, nbytes=4 * 2**20,
    )(*[keep(x) for x in (gradient, moment, block, row, owner)])


def column_halves(scr, start, slots):
    left = scr[pl.ds(2 * start, slots, stride=2), :].astype(BF)
    right = scr[pl.ds(2 * start + 1, slots, stride=2), :].astype(BF)
    return jnp.concatenate([left, right], axis=1)


def tile_kernel(
    n, got_ref, root_hbm, tile_ref, meta_ref, root_ref, scr, sem
):
    load = pltpu.make_async_copy(root_hbm, root_ref, sem)
    load.start()
    rows = tile_ref.shape[0] - EXTRA
    scr[...] = got_ref[...].astype(F32)
    meta = scr[pl.ds(2 * CAP, n, stride=2 * OUT), :]
    meta_ref[...] = meta
    col = iota((n, LANES), 1)
    adam = jnp.sum(jnp.where((col >= 32) & (col < 35), meta, 0.0), axis=(0, 1), keepdims=True)
    col = iota((EXTRA, 2 * LANES), 1)
    extra = jnp.zeros((EXTRA, 2 * LANES), F32)
    for i, piece in enumerate(split3(adam)):
        extra = jnp.where(col == i, piece.astype(F32), extra)
    tile_ref[rows:, :] = extra.astype(BF)
    by_slot = meta.T
    position = (32.0 * by_slot[0:16] + by_slot[16:32]).astype(jnp.int32)
    came = []
    for k in range(CAP):
        left = scr[pl.ds(2 * k, n, stride=2 * OUT), :].astype(BF)
        right = scr[pl.ds(2 * k + 1, n, stride=2 * OUT), :].astype(BF)
        came.append(jnp.concatenate([left, right], axis=1))
    came = jnp.concatenate(came, axis=0)
    step = rows // 4
    for start in range(0, rows, step):
        row = iota((step, n), 0) + (start + 1)
        order = [onehot(row == position[k : k + 1]) for k in range(CAP)]
        tile_ref[start : start + step, :] = dot(jnp.concatenate(order, axis=1), came).astype(BF)
    load.wait()


def tile(n, rows, got, root):
    return call(
        functools.partial(tile_kernel, n),
        (
            shape((rows + EXTRA, 2 * LANES), BF), shape((n, LANES), F32), shape(root.shape, BF),
        ),
        [VMEM, HBM],
        scratch=[pltpu.VMEM((2 * OUT * n, LANES), F32), pltpu.SemaphoreType.DMA],
        flops=2 * OUT * n * rows * 2 * LANES, nbytes=3 * 2**20,
    )(got, keep(root))


def return_order_kernel(n, meta_ref, left_hbm, order_ref, left_ref, sem):
    load = pltpu.make_async_copy(left_hbm.at[pl.ds(0, left_ref.shape[0])], left_ref, sem)
    load.start()
    rows = order_ref.shape[1]
    slots = iota((CAP * n, n), 0)
    source = iota((CAP * n, n), 1)
    expand = onehot((slots >= CAP * source) & (slots < CAP * source + CAP))
    meta = meta_ref[...]
    meta = jnp.where(iota((n, LANES), 1) < 16, 32.0 * meta, meta).astype(BF)
    by_slot = dot(expand, meta)
    which = iota((CAP * n, LANES), 0) % CAP
    lane = iota((CAP * n, LANES), 1)
    chosen = jnp.where((lane == which) | (lane == which + 16), by_slot, 0.0).astype(BF)
    position = dot(chosen, jnp.ones((LANES, LANES), BF)).astype(jnp.int32)
    lane = lane + 1
    for j in range(0, rows, LANES):
        order_ref[:, j : j + LANES] = onehot(position == lane + j)
    load.wait()


def return_order(n, rows, meta, left):
    return call(
        functools.partial(return_order_kernel, n),
        (shape((CAP * n, rows), BF), shape((3 * rows // 4, rows), BF)),
        [VMEM, HBM],
        scratch=[pltpu.SemaphoreType.DMA],
        flops=4 * CAP * n * n * LANES, nbytes=4 * 2**20,
    )(meta, keep(left))


def precond_kernel(
    n, core_ref, own_ref, other_ref, order_ref, root_own_ref, root_other_ref, left_ref,
    left_hbm, back_hbm, rest_ref, scr, back_ref, sems,
):
    rows, width = own_ref.shape[0] - EXTRA, own_ref.shape[1]
    quarter = rows // 4
    load = pltpu.make_async_copy(left_hbm.at[pl.ds(3 * quarter, quarter)], rest_ref, sems.at[CHUNKS])
    load.start()
    core = core_ref[0]
    own_rows = pl.ds(pl.multiple_of(core * width, width), width)
    other_rows = pl.ds(pl.multiple_of((1 - core) * width, width), width)
    both = jnp.concatenate([own_ref[:rows, :], other_ref[:rows, :]], axis=1)
    mixed = []
    for root_ref in (root_own_ref, root_other_ref):
        root = jnp.concatenate([root_ref[own_rows, :], root_ref[other_rows, :]], axis=0)
        mixed.append(dot(both, root).astype(BF))
    mixed_own, mixed_other = mixed
    parts, total = [], 0.0
    for i in range(4):
        if i == 3:
            load.wait()
        left = rest_ref[...] if i == 3 else left_ref[quarter * i : quarter * (i + 1), :]
        part, other_part = dot(left, mixed_own), dot(left, mixed_other)
        squares = part * part + other_part * other_part
        total = total + jnp.sum(squares.reshape(quarter // 8, 8, width), axis=0)
        parts.append(part)
    total = jnp.sum(total, axis=(0, 1), keepdims=True)
    extra = own_ref[rows:, :].astype(F32) + other_ref[rows:, :].astype(F32)
    adam = jnp.sum(extra[0:1], axis=(0, 1), keepdims=True)
    scale = jnp.sqrt(adam) / (jnp.sqrt(total) + GRAFT_EPS)
    grafted = jnp.concatenate([(part * scale).astype(BF) for part in parts], axis=0)
    part = CAP * n // CHUNKS
    stores = []
    for i in range(CHUNKS):
        chunk = pl.ds(2 * part * i, 2 * part)
        placed = dot(order_ref[part * i : part * (i + 1), :], grafted)
        scr[pl.ds(2 * part * i, part, stride=2), :] = placed[:, :LANES]
        scr[pl.ds(2 * part * i + 1, part, stride=2), :] = placed[:, LANES:]
        back_ref[chunk, :] = scr[chunk, :].astype(BF)
        store = pltpu.make_async_copy(back_ref.at[chunk], back_hbm.at[chunk], sems.at[i])
        store.start()
        stores.append(store)
    for store in stores:
        store.wait()


def precond(
    n, core, own, other, order, root_own, root_other, left_near, left
):
    rows, width = own.shape[0] - EXTRA, own.shape[1]
    return call(
        functools.partial(precond_kernel, n),
        shape((2 * CAP * n, LANES), BF),
        [SMEM] + [VMEM] * 6 + [HBM],
        HBM,
        scratch=[
            pltpu.VMEM((rows // 4, rows), BF),
            pltpu.VMEM((2 * CAP * n, LANES), F32),
            pltpu.VMEM((2 * CAP * n, LANES), BF),
            pltpu.SemaphoreType.DMA((CHUNKS + 1,)),
        ],
        flops=8 * rows * rows * width, nbytes=5 * 2**20,
    )(core, own, other, order, root_own, root_other, left_near, keep(left))


def beside_kernel(
    n, place_ref, after_ref, grad_hbm, moment_hbm, order_ref, new_hbm, grad_ref, moment_ref, sems
):
    del after_ref
    rows = order_ref.shape[0]
    loads = [
        pltpu.make_async_copy(grad_hbm, grad_ref, sems.at[0]),
        pltpu.make_async_copy(moment_hbm, moment_ref, sems.at[1]),
    ]
    for load in loads:
        load.start()
    place = jnp.broadcast_to(place_ref[...].astype(F32), (LANES, rows)).T.astype(jnp.int32)
    lane = iota((rows, LANES), 1)
    for j in range(0, CAP * n, LANES):
        order_ref[:, j : j + LANES] = onehot(place == lane + j)
    for load in loads:
        load.wait()
    moment_ref[...] = next_moment(grad_ref[...], moment_ref[...])
    store = pltpu.make_async_copy(moment_ref, new_hbm, sems.at[2])
    store.start()
    store.wait()


def beside(n, place, after, gradient, moment):
    rows, width = gradient.shape
    return call(
        functools.partial(beside_kernel, n),
        (shape((rows, CAP * n), BF), shape((rows, width), F32)),
        [VMEM, pl.BlockSpec(memory_space=pl.ANY), HBM, HBM],
        (VMEM, HBM),
        scratch=[
            pltpu.VMEM((rows, width), F32),
            pltpu.VMEM((rows, width), F32),
            pltpu.SemaphoreType.DMA((3,)),
        ],
        flops=4 * rows * width, nbytes=6 * 2**20,
    )(place, after, keep(gradient), keep(moment))


def unpack_kernel(n, back_hbm, order_ref, update_hbm, back_ref, scr, update_ref, sems):
    rows = update_ref.shape[0]
    part = CAP * n // PARTS
    loads = []
    for i in range(PARTS):
        chunk = pl.ds(2 * part * i, 2 * part)
        loads.append(pltpu.make_async_copy(back_hbm.at[chunk], back_ref.at[chunk], sems.at[i]))
        loads[i].start()
    halves = [pl.ds(i * (rows // 2), rows // 2) for i in range(2)]
    sums = [0.0, 0.0]
    for i in range(PARTS):
        chunk = pl.ds(2 * part * i, 2 * part)
        loads[i].wait()
        scr[chunk, :] = back_ref[chunk, :].astype(F32)
        came = column_halves(scr, part * i, part)
        for j, half in enumerate(halves):
            sums[j] = sums[j] + dot(order_ref[half, part * i : part * (i + 1)], came)
            if i == PARTS - 1:
                update_ref[half, :] = sums[j].astype(BF)
                store = pltpu.make_async_copy(update_ref.at[half], update_hbm.at[half], sems.at[PARTS + j])
                store.start()
                loads.append(store)
    for store in loads[PARTS:]:
        store.wait()


def unpack(n, back, order):
    rows = order.shape[0]
    return call(
        functools.partial(unpack_kernel, n),
        shape((rows, 2 * LANES), BF),
        [HBM, VMEM],
        HBM,
        scratch=[
            pltpu.VMEM((2 * CAP * n, LANES), BF),
            pltpu.VMEM((2 * CAP * n, LANES), F32),
            pltpu.VMEM((rows, 2 * LANES), BF),
            pltpu.SemaphoreType.DMA((PARTS + 2,)),
        ],
        flops=2 * CAP * n * rows * 2 * LANES, nbytes=2 * 2**20,
    )(keep(back), order)


def body(
    gradient, moment, left_stat, right_stat, left_root, right_root, seg_block, seg_row, owner_table
):
    n = lax.axis_size("dp")
    rows = gradient.shape[0]
    core = lax.axis_index("mp").astype(jnp.int32)
    swap = [(0, 1), (1, 0)]
    root_own = right_root[0]
    root_other = lax.ppermute(root_own, "mp", swap)

    send, place = pack(
        n, gradient, moment, seg_block[None, :], seg_row[None, :], owner_table[None, :]
    )
    send, root_other = lax.optimization_barrier((send, root_other))
    got = lax.all_to_all(send.reshape(n, OUT, 2, LANES), "dp", 0, 0, tiled=True)
    got = got.reshape(2 * OUT * n, LANES)
    tile_own, meta, root_near = tile(n, rows, got, root_own)
    tile_other = lax.ppermute(tile_own, "mp", swap)
    order, left_near = return_order(n, rows, meta, left_root[0])
    back = precond(
        n, core[None], tile_own, tile_other, order, root_near, root_other, left_near, left_root[0]
    )
    returned = lax.all_to_all(back.reshape(n, 2 * CAP, LANES), "dp", 0, 0, tiled=True)

    order, moment_new = beside(n, place, back, gradient, moment)
    tile_own, tile_other = tile_own[:rows], tile_other[:rows]
    whole = jnp.where(
        core == 0,
        jnp.concatenate([tile_own, tile_other], axis=1),
        jnp.concatenate([tile_other, tile_own], axis=1),
    )
    stat_rows = left_stat.shape[1]
    own_rows = lax.dynamic_slice_in_dim(whole, core * stat_rows, stat_rows, 0)
    left_new = GRAM_DECAY * left_stat[0] + dot_nt(own_rows, whole)
    right_new = GRAM_DECAY * right_stat[0] + lax.dot_general(
        tile_own, whole, (((0,), (0,)), ((), ())), preferred_element_type=F32
    )
    update = unpack(n, returned.reshape(2 * CAP * n, LANES), order)
    return (update, moment_new, left_new[None], right_new[None])


def solution(mesh):
    in_specs = (
        P("dp", "mp"),
        P("dp", "mp"),
        P("dp", "mp", None),
        P("dp", "mp", None),
        P("dp", None, None),
        P("dp", None, "mp"),
        P("dp"),
        P("dp"),
        P(),
    )
    out_specs = (P("dp", "mp"), P("dp", "mp"), P("dp", "mp", None), P("dp", "mp", None))
    return jax.shard_map(body, mesh=mesh, in_specs=in_specs, out_specs=out_specs, check_vma=False)
```

time: 92.2 us -> 91.7 us (level)
  Pallas kernels: 14.6 us -> 16.5 us
  other arithmetic: 1.81 us -> 0.26 us
    pallas_call x2, Pallas kernels: 2.23 us -> 3.9 us  [the longest x1 2.78 us: beside(): call(functools.partial(beside_kernel, n), (shape((rows, CAP * n), BF), sh...]
    select_n x1, other arithmetic: 1.81 us -> 0.26 us  [body(): jnp.where(core == 0, jnp.concatenate([tile_own, tile_other], axis=1), jnp...]
  transfers between devices with their start and end apart: 4 -> 3, of which waited for: 2 -> 2; matrix products, arithmetic and copies ran while one was open for 6% -> 4% of each run, Pallas kernels for 6% -> 8%
where the time goes in v2:
time: 91.7 us; the launch traced here: 91.4 us
  blocking collectives  42.8 us (47%)
  waiting for transfers between devices  19.2 us (21%)
  Pallas kernels  16.5 us (18%)
  starting transfers between devices  7.7 us (8%)
  matrix products  3.35 us (4%)
  between operations  0.95 us (1%)
    all_to_all x1, blocking collectives, body(): got = lax.all_to_all(send.reshape(n, OUT, 2, LANES), 'dp', 0, 0, tiled=True)  42.8 us
    all_to_all x1, waiting for transfers between devices, body(): lax.all_to_all(back.reshape(n, 2 * CAP, LANES), 'dp', 0, 0, tiled=True)  18.8 us
    all_to_all x1, starting transfers between devices, body(): lax.all_to_all(back.reshape(n, 2 * CAP, LANES), 'dp', 0, 0, tiled=True)  7.52 us
    pallas_call x1, Pallas kernels, precond(): call(functools.partial(precond_kernel, n), shape((2 * CAP * n, LANES), BF...  4.94 us
    pallas_call x1, Pallas kernels, pack(): call(functools.partial(pack_kernel, n), (shape((2 * OUT * n, LANES), BF),...  3.18 us
    pallas_call x1, Pallas kernels, unpack(): call(functools.partial(unpack_kernel, n), shape((rows, 2 * LANES), BF), [...  2.98 us
    pallas_call x1, Pallas kernels, beside(): call(functools.partial(beside_kernel, n), (shape((rows, CAP * n), BF), sh...  2.78 us
    dot_general x1, matrix products, dot_nt(): lax.dot_general(a, b, (((1,), (1,)), ((), ())), preferred_element_type=F32)  2.06 us
  transfers between devices with their start and end apart: 3, of which 2 were waited for; matrix products, arithmetic and copies ran while one was open for 4% of the time, Pallas kernels for 8%

profile of v2, /device:TPU:2, one launch (start us, length us, event | category | flops | bytes accessed | tf_op | source)
XLA Modules:
  0.0 91.4 jit_solution(12933682040990279016)
XLA Ops:
  0.6 0.1 collective-permute-start
  0.7 3.2 %shard_map.120 = (bf16[3328,128]{1,0:T(8,128)(2,1)S(1)}, s32[1,1024]{1,0:T(1,128)S(1)}) custom-call(f32[1024,256]{1,0:T(8,128)} %grad_hbm.3, f32[1024,256]{1,0:T(8,128)} %moment_hbm.3, s32[1,1024]{1,0:T(1,128)} %bitcast.27, s32[1,1024]{1,0:T(1,128)} %bitcast.28, s32[1,128]{1,0:T(1,128)} %bitcast.29), custom_call_target="tpu_custom_call" | custom-call | flops 872415232 | bytes 4194304 | tf_op jit(solution)/shard_map/pallas_call | solution.py:149
  3.9 0.0 collective-permute-done.root_other_ref
  3.9 42.8 %all_to_all.10 = bf16[128,13,2,128]{3,2,1,0:T(2,128)(2,1)S(1)} all-to-all(bf16[128,13,2,128]{3,2,1,0:T(2,128)(2,1)S(1)} %bitcast.21), channel_id=1, replica_groups=mesh['dp'=128,'mp'=2] {'dp'}, dimensions={0} | all-to-all | bytes 1703936 | tf_op jit(solution)/shard_map/all_to_all | solution.py:407
  46.7 1.1 %shard_map.121 = (bf16[1040,256]{1,0:T(8,128)(2,1)S(1)}, f32[128,128]{1,0:T(8,128)S(1)}, bf16[512,256]{1,0:T(8,128)(2,1)S(1)}) custom-call(bf16[3328,128]{1,0:T(8,128)(2,1)S(1)} %bitcast.22, bf16[512,256]{1,0:T(8,128)(2,1)} %bitcast.26), custom_call_target="tpu_custom_call" | custom-call | flops 872415232 | bytes 3145728 | tf_op jit(solution)/shard_map/pallas_call | solution.py:205
  47.9 0.0 copy-start
  47.9 0.1 collective-permute-start.1
  48.0 1.5 %shard_map.122 = (bf16[1536,1024]{1,0:T(8,128)(2,1)S(1)}, bf16[768,1024]{1,0:T(8,128)(2,1)S(1)}) custom-call(f32[128,128]{1,0:T(8,128)S(1)} %get-tuple-element.18.meta_ref, bf16[1024,1024]{1,0:T(8,128)(2,1)} %bitcast.23), custom_call_target="tpu_custom_call" | custom-call | flops 100663296 | bytes 4194304 | tf_op jit(solution)/shard_map/pallas_call | solution.py:237
  49.5 0.4 collective-permute-done.1.other_ref
  49.9 4.9 %shard_map.123.after_ref = bf16[3072,128]{1,0:T(8,128)(2,1)} custom-call(s32[1]{0:T(128)} %bitcast.core_ref, bf16[1040,256]{1,0:T(8,128)(2,1)S(1)} %get-tuple-element.17.own_ref, bf16[1040,256]{1,0:T(8,128)(2,1)S(1)} %collective-permute-done.1.other_ref, bf16[1536,1024]{1,0:T(8,128)(2,1)S(1)} %get-tuple-element.19.order_ref, ...), custom_call_target="tpu_custom_call" | custom-call | flops 2147483648 | bytes 5242880 | tf_op jit(solution)/shard_map/pallas_call | solution.py:296
  54.8 7.5 %all-to-all-start.1 = ((bf16[128,24,128]{2,1,0:T(8,128)(2,1)}), bf16[128,24,128]{2,1,0:T(8,128)(2,1)}, u32[]{:S(2)}, u32[]{:S(2)}) async-start(bf16[128,24,128]{2,1,0:T(8,128)(2,1)} %bitcast.8), calls=%async_computation.1 | async-start | bytes 1572864 | tf_op jit(solution)/shard_map/all_to_all | solution.py:415
  62.4 0.0 copy-done
  62.5 0.0 copy-start.1
  62.5 0.0 copy-start.3
  62.5 2.8 %shard_map.124 = (bf16[1024,1536]{1,0:T(8,128)(2,1)S(1)}, f32[1024,256]{1,0:T(8,128)}) custom-call(s32[1,1024]{1,0:T(1,128)S(1)} %get-tuple-element.23.place_ref, bf16[3072,128]{1,0:T(8,128)(2,1)} %shard_map.123.after_ref, f32[1024,256]{1,0:T(8,128)} %grad_hbm.3, f32[1024,256]{1,0:T(8,128)} %moment_hbm.3), custom_call_target="tpu_custom_call" | custom-call | flops 1048576 | bytes 6291456 | tf_op jit(solution)/shard_map/pallas_call | solution.py:336
  65.3 0.3 maximum_select_fusion
  65.5 0.0 copy-done.1
  65.5 0.0 copy-done.3
  65.6 0.0 copy-start.2
  65.6 1.3 %fusion.1 = f32[1,256,512]{2,1,0:T(8,128)} fusion(f32[1,256,512]{2,1,0:T(8,128)S(1)} %copy-done.3, bf16[1040,256]{1,0:T(8,128)(2,1)S(1)} %copy-done.1, bf16[1024,256]{1,0:T(8,128)(2,1)S(1)} %slice.8, bf16[1024,256]{1,0:T(8,128)(2,1)S(1)} %slice.6, pred[]{:T(512)S(6)} %eq.3), kind=kOutput, calls=%fused_computation.3 | convolution fusion | flops 273416192 | bytes 2621441 | tf_op jit(solution)/shard_map/dot_general | solution.py:427
  66.9 0.5 copy-done.2
  67.3 2.1 %fusion = f32[1,512,1024]{2,1,0:T(8,128)} fusion(f32[1,512,1024]{2,1,0:T(8,128)S(1)} %copy-done.2, bf16[1024,512]{1,0:T(8,128)(2,1)S(1)} %maximum_select_fusion, s32[]{:T(128)S(6)} %select_n.13), kind=kOutput, calls=%fused_computation.1 | convolution fusion | flops 537919488 | bytes 5767172 | tf_op jit(solution)/shard_map/dot_general | solution.py:40
  69.4 18.8 %all-to-all-done.1 = bf16[128,24,128]{2,1,0:T(8,128)(2,1)} async-done(((bf16[128,24,128]{2,1,0:T(8,128)(2,1)}), bf16[128,24,128]{2,1,0:T(8,128)(2,1)}, u32[]{:S(2)}, u32[]{:S(2)}) %all-to-all-start.1) | async-done | bytes 786464 | tf_op jit(solution)/shard_map/all_to_all | solution.py:415
  88.2 3.0 %shard_map.125 = bf16[1024,256]{1,0:T(8,128)(2,1)} custom-call(bf16[3072,128]{1,0:T(8,128)(2,1)} %bitcast.9.back_hbm, bf16[1024,1536]{1,0:T(8,128)(2,1)S(1)} %get-tuple-element.24.order_ref), custom_call_target="tpu_custom_call" | custom-call | flops 805306368 | bytes 2097152 | tf_op jit(solution)/shard_map/pallas_call | solution.py:378
  (2 shorter events, 0.1 us)
Async XLA Ops:
  0.6 3.3 %collective-permute-start = (bf16[512,256]{1,0:T(8,128)(2,1)}, bf16[512,256]{1,0:T(8,128)(2,1)S(1)}, u32[]{:S(2)}, u32[]{:S(2)}) collective-permute-start(bf16[512,256]{1,0:T(8,128)(2,1)} %bitcast.25), channel_id=1, source_target_pairs={{0,1},{1,0},{2,3},{3,2},{4,5},{5,4},{6,7},{7,6},{8,9},{9,8},{10,11... | collective-permute-start | bytes 786440 | tf_op jit(solution)/shard_map/ppermute | solution.py:401
  47.9 14.5 %copy-start = (bf16[1040,256]{1,0:T(8,128)(2,1)}, bf16[1040,256]{1,0:T(8,128)(2,1)S(1)}, u32[]{:S(2)}) copy-start(bf16[1040,256]{1,0:T(8,128)(2,1)S(1)} %get-tuple-element.17.own_ref) | copy-start | bytes 1597444
  47.9 2.0 %collective-permute-start.1 = (bf16[1040,256]{1,0:T(8,128)(2,1)S(1)}, bf16[1040,256]{1,0:T(8,128)(2,1)S(1)}, u32[]{:S(2)}, u32[]{:S(2)}) collective-permute-start(bf16[1040,256]{1,0:T(8,128)(2,1)S(1)} %get-tuple-element.17.own_ref), channel_id=1, source_target_pairs={{0,1},{1,0},{2,3},{3,2},{4,5},{5,4},{6,7},{7,6},{8,9},{9,8},{10,11... | collective-permute-start | bytes 1597448 | tf_op jit(solution)/shard_map/ppermute | solution.py:410
  54.8 33.4 %all-to-all-start.1 = ((bf16[128,24,128]{2,1,0:T(8,128)(2,1)}), bf16[128,24,128]{2,1,0:T(8,128)(2,1)}, u32[]{:S(2)}, u32[]{:S(2)}) async-start(bf16[128,24,128]{2,1,0:T(8,128)(2,1)} %bitcast.8), calls=%async_computation.1 | async-start | bytes 1572864 | tf_op jit(solution)/shard_map/all_to_all | solution.py:415
  62.5 3.1 %copy-start.1 = (bf16[1040,256]{1,0:T(8,128)(2,1)S(1)}, bf16[1040,256]{1,0:T(8,128)(2,1)}, u32[]{:S(2)}) copy-start(bf16[1040,256]{1,0:T(8,128)(2,1)} %copy-done) | copy-start | bytes 1597444
  62.5 3.1 %copy-start.3 = (f32[1,256,512]{2,1,0:T(8,128)S(1)}, f32[1,256,512]{2,1,0:T(8,128)}, u32[]{:S(2)}) copy-start(f32[1,256,512]{2,1,0:T(8,128)} %param.12) | copy-start | bytes 1572868
  65.6 1.8 %copy-start.2 = (f32[1,512,1024]{2,1,0:T(8,128)S(1)}, f32[1,512,1024]{2,1,0:T(8,128)}, u32[]{:S(2)}) copy-start(f32[1,512,1024]{2,1,0:T(8,128)} %param.11) | copy-start | bytes 6291460

commit v3 on v2

--- a/solution.py
+++ b/solution.py
@@ -214,7 +214,7 @@
 
 
 def return_order_kernel(n, meta_ref, left_hbm, order_ref, left_ref, sem):
-    load = pltpu.make_async_copy(left_hbm.at[pl.ds(0, left_ref.shape[0])], left_ref, sem)
+    load = pltpu.make_async_copy(left_hbm, left_ref, sem)
     load.start()
     rows = order_ref.shape[1]
     slots = iota((CAP * n, n), 0)
@@ -236,7 +236,7 @@
 def return_order(n, rows, meta, left):
     return call(
         functools.partial(return_order_kernel, n),
-        (shape((CAP * n, rows), BF), shape((3 * rows // 4, rows), BF)),
+        (shape((CAP * n, rows), BF), shape((rows, rows), BF)),
         [VMEM, HBM],
         scratch=[pltpu.SemaphoreType.DMA],
         flops=4 * CAP * n * n * LANES, nbytes=4 * 2**20,
@@ -245,12 +245,10 @@
 
 def precond_kernel(
     n, core_ref, own_ref, other_ref, order_ref, root_own_ref, root_other_ref, left_ref,
-    left_hbm, back_hbm, rest_ref, scr, back_ref, sems,
+    back_hbm, scr, back_ref, sems,
 ):
     rows, width = own_ref.shape[0] - EXTRA, own_ref.shape[1]
     quarter = rows // 4
-    load = pltpu.make_async_copy(left_hbm.at[pl.ds(3 * quarter, quarter)], rest_ref, sems.at[CHUNKS])
-    load.start()
     core = core_ref[0]
     own_rows = pl.ds(pl.multiple_of(core * width, width), width)
     other_rows = pl.ds(pl.multiple_of((1 - core) * width, width), width)
@@ -262,9 +260,7 @@
     mixed_own, mixed_other = mixed
     parts, total = [], 0.0
     for i in range(4):
-        if i == 3:
-            load.wait()
-        left = rest_ref[...] if i == 3 else left_ref[quarter * i : quarter * (i + 1), :]
+        left = left_ref[quarter * i : quarter * (i + 1), :]
         part, other_part = dot(left, mixed_own), dot(left, mixed_other)
         squares = part * part + other_part * other_part
         total = total + jnp.sum(squares.reshape(quarter // 8, 8, width), axis=0)
@@ -290,22 +286,21 @@
 
 
 def precond(
-    n, core, own, other, order, root_own, root_other, left_near, left
+    n, core, own, other, order, root_own, root_other, left
 ):
     rows, width = own.shape[0] - EXTRA, own.shape[1]
     return call(
         functools.partial(precond_kernel, n),
         shape((2 * CAP * n, LANES), BF),
-        [SMEM] + [VMEM] * 6 + [HBM],
+        [SMEM] + [VMEM] * 6,
         HBM,
         scratch=[
-            pltpu.VMEM((rows // 4, rows), BF),
             pltpu.VMEM((2 * CAP * n, LANES), F32),
             pltpu.VMEM((2 * CAP * n, LANES), BF),
-            pltpu.SemaphoreType.DMA((CHUNKS + 1,)),
+            pltpu.SemaphoreType.DMA((CHUNKS,)),
         ],
         flops=8 * rows * rows * width, nbytes=5 * 2**20,
-    )(core, own, other, order, root_own, root_other, left_near, keep(left))
+    )(core, own, other, order, root_own, root_other, left)
 
 
 def beside_kernel(
@@ -408,9 +403,9 @@
     got = got.reshape(2 * OUT * n, LANES)
     tile_own, meta, root_near = tile(n, rows, got, root_own)
     tile_other = lax.ppermute(tile_own, "mp", swap)
-    order, left_near = return_order(n, rows, meta, left_root[0])
+    order, left = return_order(n, rows, meta, left_root[0])
     back = precond(
-        n, core[None], tile_own, tile_other, order, root_near, root_other, left_near, left_root[0]
+        n, core[None], tile_own, tile_other, order, root_near, root_other, left
     )
     returned = lax.all_to_all(back.reshape(n, 2 * CAP, LANES), "dp", 0, 0, tiled=True)
 

time: 91.7 us -> 90.7 us (0.989)
    pallas_call x1, Pallas kernels: 4.94 us -> 3.88 us  [precond(): call(functools.partial(precond_kernel, n), shape((2 * CAP * n, LANES), BF...]
where the time goes in v3:
time: 90.7 us; the launch traced here: 90.4 us
  blocking collectives  42.8 us (47%)
  waiting for transfers between devices  19.1 us (21%)
  Pallas kernels  15.6 us (17%)
  starting transfers between devices  7.7 us (8%)
  matrix products  3.35 us (4%)
  between operations  0.95 us (1%)
    all_to_all x1, blocking collectives, body(): got = lax.all_to_all(send.reshape(n, OUT, 2, LANES), 'dp', 0, 0, tiled=True)  42.8 us
    all_to_all x1, waiting for transfers between devices, body(): lax.all_to_all(back.reshape(n, 2 * CAP, LANES), 'dp', 0, 0, tiled=True)  18.9 us
    all_to_all x1, starting transfers between devices, body(): lax.all_to_all(back.reshape(n, 2 * CAP, LANES), 'dp', 0, 0, tiled=True)  7.51 us
    pallas_call x1, Pallas kernels, precond(): call(functools.partial(precond_kernel, n), shape((2 * CAP * n, LANES), BF...  3.88 us
    pallas_call x1, Pallas kernels, pack(): call(functools.partial(pack_kernel, n), (shape((2 * OUT * n, LANES), BF),...  3.18 us
    pallas_call x1, Pallas kernels, unpack(): call(functools.partial(unpack_kernel, n), shape((rows, 2 * LANES), BF), [...  2.99 us
    pallas_call x1, Pallas kernels, beside(): call(functools.partial(beside_kernel, n), (shape((rows, CAP * n), BF), sh...  2.78 us
    dot_general x1, matrix products, dot_nt(): lax.dot_general(a, b, (((1,), (1,)), ((), ())), preferred_element_type=F32)  2.06 us
  transfers between devices with their start and end apart: 3, of which 2 were waited for; matrix products, arithmetic and copies ran while one was open for 4% of the time, Pallas kernels for 8%

profile of v3, /device:TPU:2, one launch (start us, length us, event | category | flops | bytes accessed | tf_op | source)
XLA Modules:
  0.0 90.4 jit_solution(14651377549223700868)
XLA Ops:
  0.6 0.1 collective-permute-start
  0.7 3.2 %shard_map.120 = (bf16[3328,128]{1,0:T(8,128)(2,1)S(1)}, s32[1,1024]{1,0:T(1,128)S(1)}) custom-call(f32[1024,256]{1,0:T(8,128)} %grad_hbm.3, f32[1024,256]{1,0:T(8,128)} %moment_hbm.3, s32[1,1024]{1,0:T(1,128)} %bitcast.26, s32[1,1024]{1,0:T(1,128)} %bitcast.27, s32[1,128]{1,0:T(1,128)} %bitcast.28), custom_call_target="tpu_custom_call" | custom-call | flops 872415232 | bytes 4194304 | tf_op jit(solution)/shard_map/pallas_call | solution.py:149
  3.9 0.0 collective-permute-done.root_other_ref
  3.9 42.8 %all_to_all.10 = bf16[128,13,2,128]{3,2,1,0:T(2,128)(2,1)S(1)} all-to-all(bf16[128,13,2,128]{3,2,1,0:T(2,128)(2,1)S(1)} %bitcast.21), channel_id=1, replica_groups=mesh['dp'=128,'mp'=2] {'dp'}, dimensions={0} | all-to-all | bytes 1703936 | tf_op jit(solution)/shard_map/all_to_all | solution.py:402
  46.7 1.1 %shard_map.121 = (bf16[1040,256]{1,0:T(8,128)(2,1)S(1)}, f32[128,128]{1,0:T(8,128)S(1)}, bf16[512,256]{1,0:T(8,128)(2,1)S(1)}) custom-call(bf16[3328,128]{1,0:T(8,128)(2,1)S(1)} %bitcast.22, bf16[512,256]{1,0:T(8,128)(2,1)} %bitcast.25), custom_call_target="tpu_custom_call" | custom-call | flops 872415232 | bytes 3145728 | tf_op jit(solution)/shard_map/pallas_call | solution.py:205
  47.9 0.0 copy-start
  47.9 0.1 collective-permute-start.1
  48.0 1.7 %shard_map.122 = (bf16[1536,1024]{1,0:T(8,128)(2,1)S(1)}, bf16[1024,1024]{1,0:T(8,128)(2,1)S(1)}) custom-call(f32[128,128]{1,0:T(8,128)S(1)} %get-tuple-element.18.meta_ref, bf16[1024,1024]{1,0:T(8,128)(2,1)} %bitcast.23), custom_call_target="tpu_custom_call" | custom-call | flops 100663296 | bytes 4194304 | tf_op jit(solution)/shard_map/pallas_call | solution.py:237
  49.7 0.2 collective-permute-done.1.other_ref
  49.9 3.9 %shard_map.123.after_ref = bf16[3072,128]{1,0:T(8,128)(2,1)} custom-call(s32[1]{0:T(128)} %bitcast.core_ref, bf16[1040,256]{1,0:T(8,128)(2,1)S(1)} %get-tuple-element.17.own_ref, bf16[1040,256]{1,0:T(8,128)(2,1)S(1)} %collective-permute-done.1.other_ref, bf16[1536,1024]{1,0:T(8,128)(2,1)S(1)} %get-tuple-element.19.order_ref, ...), custom_call_target="tpu_custom_call" | custom-call | flops 2147483648 | bytes 5242880 | tf_op jit(solution)/shard_map/pallas_call | solution.py:292
  53.8 7.5 %all-to-all-start.1 = ((bf16[128,24,128]{2,1,0:T(8,128)(2,1)}), bf16[128,24,128]{2,1,0:T(8,128)(2,1)}, u32[]{:S(2)}, u32[]{:S(2)}) async-start(bf16[128,24,128]{2,1,0:T(8,128)(2,1)} %bitcast.8), calls=%async_computation.1 | async-start | bytes 1572864 | tf_op jit(solution)/shard_map/all_to_all | solution.py:410
  61.3 0.0 copy-done
  61.4 0.0 copy-start.1
  61.4 0.0 copy-start.3
  61.4 2.8 %shard_map.124 = (bf16[1024,1536]{1,0:T(8,128)(2,1)S(1)}, f32[1024,256]{1,0:T(8,128)}) custom-call(s32[1,1024]{1,0:T(1,128)S(1)} %get-tuple-element.23.place_ref, bf16[3072,128]{1,0:T(8,128)(2,1)} %shard_map.123.after_ref, f32[1024,256]{1,0:T(8,128)} %grad_hbm.3, f32[1024,256]{1,0:T(8,128)} %moment_hbm.3), custom_call_target="tpu_custom_call" | custom-call | flops 1048576 | bytes 6291456 | tf_op jit(solution)/shard_map/pallas_call | solution.py:331
  64.2 0.3 maximum_select_fusion
  64.5 0.0 copy-done.1
  64.5 0.0 copy-done.3
  64.5 0.0 copy-start.2
  64.5 1.3 %fusion.1 = f32[1,256,512]{2,1,0:T(8,128)} fusion(f32[1,256,512]{2,1,0:T(8,128)S(1)} %copy-done.3, bf16[1040,256]{1,0:T(8,128)(2,1)S(1)} %copy-done.1, bf16[1024,256]{1,0:T(8,128)(2,1)S(1)} %slice.8, bf16[1024,256]{1,0:T(8,128)(2,1)S(1)} %slice.6, pred[]{:T(512)S(6)} %eq.3), kind=kOutput, calls=%fused_computation.3 | convolution fusion | flops 273416192 | bytes 2621441 | tf_op jit(solution)/shard_map/dot_general | solution.py:422
  65.8 0.5 copy-done.2
  66.3 2.1 %fusion = f32[1,512,1024]{2,1,0:T(8,128)} fusion(f32[1,512,1024]{2,1,0:T(8,128)S(1)} %copy-done.2, bf16[1024,512]{1,0:T(8,128)(2,1)S(1)} %maximum_select_fusion, s32[]{:T(128)S(6)} %select_n.13), kind=kOutput, calls=%fused_computation.1 | convolution fusion | flops 537919488 | bytes 5767172 | tf_op jit(solution)/shard_map/dot_general | solution.py:40
  68.3 18.9 %all-to-all-done.1 = bf16[128,24,128]{2,1,0:T(8,128)(2,1)} async-done(((bf16[128,24,128]{2,1,0:T(8,128)(2,1)}), bf16[128,24,128]{2,1,0:T(8,128)(2,1)}, u32[]{:S(2)}, u32[]{:S(2)}) %all-to-all-start.1) | async-done | bytes 786464 | tf_op jit(solution)/shard_map/all_to_all | solution.py:410
  87.2 3.0 %shard_map.125 = bf16[1024,256]{1,0:T(8,128)(2,1)} custom-call(bf16[3072,128]{1,0:T(8,128)(2,1)} %bitcast.9.back_hbm, bf16[1024,1536]{1,0:T(8,128)(2,1)S(1)} %get-tuple-element.24.order_ref), custom_call_target="tpu_custom_call" | custom-call | flops 805306368 | bytes 2097152 | tf_op jit(solution)/shard_map/pallas_call | solution.py:373
  (2 shorter events, 0.1 us)
Async XLA Ops:
  0.6 3.3 %collective-permute-start = (bf16[512,256]{1,0:T(8,128)(2,1)}, bf16[512,256]{1,0:T(8,128)(2,1)S(1)}, u32[]{:S(2)}, u32[]{:S(2)}) collective-permute-start(bf16[512,256]{1,0:T(8,128)(2,1)} %bitcast.24), channel_id=1, source_target_pairs={{0,1},{1,0},{2,3},{3,2},{4,5},{5,4},{6,7},{7,6},{8,9},{9,8},{10,11... | collective-permute-start | bytes 786440 | tf_op jit(solution)/shard_map/ppermute | solution.py:396
  47.9 13.4 %copy-start = (bf16[1040,256]{1,0:T(8,128)(2,1)}, bf16[1040,256]{1,0:T(8,128)(2,1)S(1)}, u32[]{:S(2)}) copy-start(bf16[1040,256]{1,0:T(8,128)(2,1)S(1)} %get-tuple-element.17.own_ref) | copy-start | bytes 1597444
  47.9 2.0 %collective-permute-start.1 = (bf16[1040,256]{1,0:T(8,128)(2,1)S(1)}, bf16[1040,256]{1,0:T(8,128)(2,1)S(1)}, u32[]{:S(2)}, u32[]{:S(2)}) collective-permute-start(bf16[1040,256]{1,0:T(8,128)(2,1)S(1)} %get-tuple-element.17.own_ref), channel_id=1, source_target_pairs={{0,1},{1,0},{2,3},{3,2},{4,5},{5,4},{6,7},{7,6},{8,9},{9,8},{10,11... | collective-permute-start | bytes 1597448 | tf_op jit(solution)/shard_map/ppermute | solution.py:405
  53.8 33.5 %all-to-all-start.1 = ((bf16[128,24,128]{2,1,0:T(8,128)(2,1)}), bf16[128,24,128]{2,1,0:T(8,128)(2,1)}, u32[]{:S(2)}, u32[]{:S(2)}) async-start(bf16[128,24,128]{2,1,0:T(8,128)(2,1)} %bitcast.8), calls=%async_computation.1 | async-start | bytes 1572864 | tf_op jit(solution)/shard_map/all_to_all | solution.py:410
  61.4 3.1 %copy-start.1 = (bf16[1040,256]{1,0:T(8,128)(2,1)S(1)}, bf16[1040,256]{1,0:T(8,128)(2,1)}, u32[]{:S(2)}) copy-start(bf16[1040,256]{1,0:T(8,128)(2,1)} %copy-done) | copy-start | bytes 1597444
  61.4 3.1 %copy-start.3 = (f32[1,256,512]{2,1,0:T(8,128)S(1)}, f32[1,256,512]{2,1,0:T(8,128)}, u32[]{:S(2)}) copy-start(f32[1,256,512]{2,1,0:T(8,128)} %param.12) | copy-start | bytes 1572868
  64.5 1.8 %copy-start.2 = (f32[1,512,1024]{2,1,0:T(8,128)S(1)}, f32[1,512,1024]{2,1,0:T(8,128)}, u32[]{:S(2)}) copy-start(f32[1,512,1024]{2,1,0:T(8,128)} %param.11) | copy-start | bytes 6291460

commit v4 on v3

--- a/solution.py
+++ b/solution.py
@@ -22,6 +22,7 @@
 LOADS = 2
 CHUNKS = 4
 PARTS = 3
+STORES = 4
 VMEM = pl.BlockSpec(memory_space=pltpu.VMEM)
 SMEM = pl.BlockSpec(memory_space=pltpu.SMEM)
 HBM = pl.BlockSpec(memory_space=pltpu.HBM)
@@ -350,18 +351,18 @@
         chunk = pl.ds(2 * part * i, 2 * part)
         loads.append(pltpu.make_async_copy(back_hbm.at[chunk], back_ref.at[chunk], sems.at[i]))
         loads[i].start()
-    halves = [pl.ds(i * (rows // 2), rows // 2) for i in range(2)]
-    sums = [0.0, 0.0]
+    groups = [pl.ds(i * (rows // STORES), rows // STORES) for i in range(STORES)]
+    sums = [0.0] * STORES
     for i in range(PARTS):
         chunk = pl.ds(2 * part * i, 2 * part)
         loads[i].wait()
         scr[chunk, :] = back_ref[chunk, :].astype(F32)
         came = column_halves(scr, part * i, part)
-        for j, half in enumerate(halves):
-            sums[j] = sums[j] + dot(order_ref[half, part * i : part * (i + 1)], came)
+        for j, group in enumerate(groups):
+            sums[j] = sums[j] + dot(order_ref[group, part * i : part * (i + 1)], came)
             if i == PARTS - 1:
-                update_ref[half, :] = sums[j].astype(BF)
-                store = pltpu.make_async_copy(update_ref.at[half], update_hbm.at[half], sems.at[PARTS + j])
+                update_ref[group, :] = sums[j].astype(BF)
+                store = pltpu.make_async_copy(update_ref.at[group], update_hbm.at[group], sems.at[PARTS + j])
                 store.start()
                 loads.append(store)
     for store in loads[PARTS:]:
@@ -379,7 +380,7 @@
             pltpu.VMEM((2 * CAP * n, LANES), BF),
             pltpu.VMEM((2 * CAP * n, LANES), F32),
             pltpu.VMEM((rows, 2 * LANES), BF),
-            pltpu.SemaphoreType.DMA((PARTS + 2,)),
+            pltpu.SemaphoreType.DMA((PARTS + STORES,)),
         ],
         flops=2 * CAP * n * rows * 2 * LANES, nbytes=2 * 2**20,
     )(keep(back), order)

time: 90.7 us -> 90.6 us (level)
  no operation moved by 1% of the time
where the time goes in v4:
time: 90.6 us; the launch traced here: 90.3 us
  blocking collectives  42.8 us (47%)
  waiting for transfers between devices  19.1 us (21%)
  Pallas kernels  15.5 us (17%)
  starting transfers between devices  7.7 us (8%)
  matrix products  3.35 us (4%)
  between operations  0.95 us (1%)
    all_to_all x1, blocking collectives, body(): got = lax.all_to_all(send.reshape(n, OUT, 2, LANES), 'dp', 0, 0, tiled=True)  42.8 us
    all_to_all x1, waiting for transfers between devices, body(): lax.all_to_all(back.reshape(n, 2 * CAP, LANES), 'dp', 0, 0, tiled=True)  18.9 us
    all_to_all x1, starting transfers between devices, body(): lax.all_to_all(back.reshape(n, 2 * CAP, LANES), 'dp', 0, 0, tiled=True)  7.51 us
    pallas_call x1, Pallas kernels, precond(): call(functools.partial(precond_kernel, n), shape((2 * CAP * n, LANES), BF...  3.88 us
    pallas_call x1, Pallas kernels, pack(): call(functools.partial(pack_kernel, n), (shape((2 * OUT * n, LANES), BF),...  3.18 us
    pallas_call x1, Pallas kernels, unpack(): call(functools.partial(unpack_kernel, n), shape((rows, 2 * LANES), BF), [...  2.89 us
    pallas_call x1, Pallas kernels, beside(): call(functools.partial(beside_kernel, n), (shape((rows, CAP * n), BF), sh...  2.78 us
    dot_general x1, matrix products, dot_nt(): lax.dot_general(a, b, (((1,), (1,)), ((), ())), preferred_element_type=F32)  2.06 us
  transfers between devices with their start and end apart: 3, of which 2 were waited for; matrix products, arithmetic and copies ran while one was open for 4% of the time, Pallas kernels for 8%

profile of v4, /device:TPU:2, one launch (start us, length us, event | category | flops | bytes accessed | tf_op | source)
XLA Modules:
  0.0 90.3 jit_solution(4700653338164375309)
XLA Ops:
  0.6 0.1 collective-permute-start
  0.7 3.2 %shard_map.120 = (bf16[3328,128]{1,0:T(8,128)(2,1)S(1)}, s32[1,1024]{1,0:T(1,128)S(1)}) custom-call(f32[1024,256]{1,0:T(8,128)} %grad_hbm.3, f32[1024,256]{1,0:T(8,128)} %moment_hbm.3, s32[1,1024]{1,0:T(1,128)} %bitcast.26, s32[1,1024]{1,0:T(1,128)} %bitcast.27, s32[1,128]{1,0:T(1,128)} %bitcast.28), custom_call_target="tpu_custom_call" | custom-call | flops 872415232 | bytes 4194304 | tf_op jit(solution)/shard_map/pallas_call | solution.py:150
  3.9 0.0 collective-permute-done.root_other_ref
  3.9 42.8 %all_to_all.10 = bf16[128,13,2,128]{3,2,1,0:T(2,128)(2,1)S(1)} all-to-all(bf16[128,13,2,128]{3,2,1,0:T(2,128)(2,1)S(1)} %bitcast.21), channel_id=1, replica_groups=mesh['dp'=128,'mp'=2] {'dp'}, dimensions={0} | all-to-all | bytes 1703936 | tf_op jit(solution)/shard_map/all_to_all | solution.py:403
  46.7 1.1 %shard_map.121 = (bf16[1040,256]{1,0:T(8,128)(2,1)S(1)}, f32[128,128]{1,0:T(8,128)S(1)}, bf16[512,256]{1,0:T(8,128)(2,1)S(1)}) custom-call(bf16[3328,128]{1,0:T(8,128)(2,1)S(1)} %bitcast.22, bf16[512,256]{1,0:T(8,128)(2,1)} %bitcast.25), custom_call_target="tpu_custom_call" | custom-call | flops 872415232 | bytes 3145728 | tf_op jit(solution)/shard_map/pallas_call | solution.py:206
  47.9 0.0 copy-start
  47.9 0.1 collective-permute-start.1
  48.0 1.7 %shard_map.122 = (bf16[1536,1024]{1,0:T(8,128)(2,1)S(1)}, bf16[1024,1024]{1,0:T(8,128)(2,1)S(1)}) custom-call(f32[128,128]{1,0:T(8,128)S(1)} %get-tuple-element.18.meta_ref, bf16[1024,1024]{1,0:T(8,128)(2,1)} %bitcast.23), custom_call_target="tpu_custom_call" | custom-call | flops 100663296 | bytes 4194304 | tf_op jit(solution)/shard_map/pallas_call | solution.py:238
  49.7 0.2 collective-permute-done.1.other_ref
  49.9 3.9 %shard_map.123.after_ref = bf16[3072,128]{1,0:T(8,128)(2,1)} custom-call(s32[1]{0:T(128)} %bitcast.core_ref, bf16[1040,256]{1,0:T(8,128)(2,1)S(1)} %get-tuple-element.17.own_ref, bf16[1040,256]{1,0:T(8,128)(2,1)S(1)} %collective-permute-done.1.other_ref, bf16[1536,1024]{1,0:T(8,128)(2,1)S(1)} %get-tuple-element.19.order_ref, ...), custom_call_target="tpu_custom_call" | custom-call | flops 2147483648 | bytes 5242880 | tf_op jit(solution)/shard_map/pallas_call | solution.py:293
  53.8 7.5 %all-to-all-start.1 = ((bf16[128,24,128]{2,1,0:T(8,128)(2,1)}), bf16[128,24,128]{2,1,0:T(8,128)(2,1)}, u32[]{:S(2)}, u32[]{:S(2)}) async-start(bf16[128,24,128]{2,1,0:T(8,128)(2,1)} %bitcast.8), calls=%async_computation.1 | async-start | bytes 1572864 | tf_op jit(solution)/shard_map/all_to_all | solution.py:411
  61.3 0.0 copy-done
  61.4 0.0 copy-start.1
  61.4 0.0 copy-start.3
  61.4 2.8 %shard_map.124 = (bf16[1024,1536]{1,0:T(8,128)(2,1)S(1)}, f32[1024,256]{1,0:T(8,128)}) custom-call(s32[1,1024]{1,0:T(1,128)S(1)} %get-tuple-element.23.place_ref, bf16[3072,128]{1,0:T(8,128)(2,1)} %shard_map.123.after_ref, f32[1024,256]{1,0:T(8,128)} %grad_hbm.3, f32[1024,256]{1,0:T(8,128)} %moment_hbm.3), custom_call_target="tpu_custom_call" | custom-call | flops 1048576 | bytes 6291456 | tf_op jit(solution)/shard_map/pallas_call | solution.py:332
  64.2 0.3 maximum_select_fusion
  64.5 0.0 copy-done.1
  64.5 0.0 copy-done.3
  64.5 0.0 copy-start.2
  64.5 1.3 %fusion.1 = f32[1,256,512]{2,1,0:T(8,128)} fusion(f32[1,256,512]{2,1,0:T(8,128)S(1)} %copy-done.3, bf16[1040,256]{1,0:T(8,128)(2,1)S(1)} %copy-done.1, bf16[1024,256]{1,0:T(8,128)(2,1)S(1)} %slice.8, bf16[1024,256]{1,0:T(8,128)(2,1)S(1)} %slice.6, pred[]{:T(512)S(6)} %eq.3), kind=kOutput, calls=%fused_computation.3 | convolution fusion | flops 273416192 | bytes 2621441 | tf_op jit(solution)/shard_map/dot_general | solution.py:423
  65.8 0.5 copy-done.2
  66.3 2.1 %fusion = f32[1,512,1024]{2,1,0:T(8,128)} fusion(f32[1,512,1024]{2,1,0:T(8,128)S(1)} %copy-done.2, bf16[1024,512]{1,0:T(8,128)(2,1)S(1)} %maximum_select_fusion, s32[]{:T(128)S(6)} %select_n.13), kind=kOutput, calls=%fused_computation.1 | convolution fusion | flops 537919488 | bytes 5767172 | tf_op jit(solution)/shard_map/dot_general | solution.py:41
  68.3 18.9 %all-to-all-done.1 = bf16[128,24,128]{2,1,0:T(8,128)(2,1)} async-done(((bf16[128,24,128]{2,1,0:T(8,128)(2,1)}), bf16[128,24,128]{2,1,0:T(8,128)(2,1)}, u32[]{:S(2)}, u32[]{:S(2)}) %all-to-all-start.1) | async-done | bytes 786464 | tf_op jit(solution)/shard_map/all_to_all | solution.py:411
  87.2 2.9 %shard_map.125 = bf16[1024,256]{1,0:T(8,128)(2,1)} custom-call(bf16[3072,128]{1,0:T(8,128)(2,1)} %bitcast.9.back_hbm, bf16[1024,1536]{1,0:T(8,128)(2,1)S(1)} %get-tuple-element.24.order_ref), custom_call_target="tpu_custom_call" | custom-call | flops 805306368 | bytes 2097152 | tf_op jit(solution)/shard_map/pallas_call | solution.py:374
  (2 shorter events, 0.1 us)
Async XLA Ops:
  0.6 3.3 %collective-permute-start = (bf16[512,256]{1,0:T(8,128)(2,1)}, bf16[512,256]{1,0:T(8,128)(2,1)S(1)}, u32[]{:S(2)}, u32[]{:S(2)}) collective-permute-start(bf16[512,256]{1,0:T(8,128)(2,1)} %bitcast.24), channel_id=1, source_target_pairs={{0,1},{1,0},{2,3},{3,2},{4,5},{5,4},{6,7},{7,6},{8,9},{9,8},{10,11... | collective-permute-start | bytes 786440 | tf_op jit(solution)/shard_map/ppermute | solution.py:397
  47.9 13.4 %copy-start = (bf16[1040,256]{1,0:T(8,128)(2,1)}, bf16[1040,256]{1,0:T(8,128)(2,1)S(1)}, u32[]{:S(2)}) copy-start(bf16[1040,256]{1,0:T(8,128)(2,1)S(1)} %get-tuple-element.17.own_ref) | copy-start | bytes 1597444
  47.9 2.0 %collective-permute-start.1 = (bf16[1040,256]{1,0:T(8,128)(2,1)S(1)}, bf16[1040,256]{1,0:T(8,128)(2,1)S(1)}, u32[]{:S(2)}, u32[]{:S(2)}) collective-permute-start(bf16[1040,256]{1,0:T(8,128)(2,1)S(1)} %get-tuple-element.17.own_ref), channel_id=1, source_target_pairs={{0,1},{1,0},{2,3},{3,2},{4,5},{5,4},{6,7},{7,6},{8,9},{9,8},{10,11... | collective-permute-start | bytes 1597448 | tf_op jit(solution)/shard_map/ppermute | solution.py:406
  53.8 33.5 %all-to-all-start.1 = ((bf16[128,24,128]{2,1,0:T(8,128)(2,1)}), bf16[128,24,128]{2,1,0:T(8,128)(2,1)}, u32[]{:S(2)}, u32[]{:S(2)}) async-start(bf16[128,24,128]{2,1,0:T(8,128)(2,1)} %bitcast.8), calls=%async_computation.1 | async-start | bytes 1572864 | tf_op jit(solution)/shard_map/all_to_all | solution.py:411
  61.4 3.1 %copy-start.1 = (bf16[1040,256]{1,0:T(8,128)(2,1)S(1)}, bf16[1040,256]{1,0:T(8,128)(2,1)}, u32[]{:S(2)}) copy-start(bf16[1040,256]{1,0:T(8,128)(2,1)} %copy-done) | copy-start | bytes 1597444
  61.4 3.1 %copy-start.3 = (f32[1,256,512]{2,1,0:T(8,128)S(1)}, f32[1,256,512]{2,1,0:T(8,128)}, u32[]{:S(2)}) copy-start(f32[1,256,512]{2,1,0:T(8,128)} %param.12) | copy-start | bytes 1572868
  64.5 1.8 %copy-start.2 = (f32[1,512,1024]{2,1,0:T(8,128)S(1)}, f32[1,512,1024]{2,1,0:T(8,128)}, u32[]{:S(2)}) copy-start(f32[1,512,1024]{2,1,0:T(8,128)} %param.11) | copy-start | bytes 6291460
